TPU v7x, 128 devices: a whole 4x4x4 slice. The times are simulated.
128 devices in a mesh: dp: 8 (over z_lo, y), fsdp: 16 (over z_hi, x, core).
Axes of the slice: x: 4, y: 4, z: 4 (z_hi: 2, z_lo: 2; z = z_hi * 2 + z_lo), core: 2. Of those that a mesh axis runs over, the one named last changes fastest.
Arguments:
- queries: bfloat16 [16384, 4096], P(('dp', 'fsdp')), may hold values from -70 to 70
- keys: bfloat16 [16384, 512], P(('dp', 'fsdp')), may hold values from -6 to 6
- values: bfloat16 [16384, 512], P(('dp', 'fsdp')), may hold values from -6 to 6
- output_gradient: bfloat16 [16384, 4096], P(('dp', 'fsdp')), may hold values from -6 to 6
- doc_lengths: int32 [8, 8], replicated, may hold values from 1 to 1024, 2048 in all within a row
- block_order: int32 [8, 128], replicated, may hold values from 0 to 127, each once within a row
- group_shift: int32 [16, 8], replicated, may hold values from 0 to 7, each once within a row
Outputs:
- attn_out: bfloat16 [16384, 4096], P(('dp', 'fsdp'))
- grad_q: bfloat16 [16384, 4096], P(('dp', 'fsdp'))
- grad_k: bfloat16 [16384, 512], P(('dp', 'fsdp'))
- grad_v: bfloat16 [16384, 512], P(('dp', 'fsdp'))
Inputs may be any that keep to these rules, and one draw needn't show every extreme that they name: `doc_lengths`: each row holds the lengths of the 8 documents of one group in position order; a row sums to 2048 and its largest entry is 1024. `block_order`: each row is a permutation. `group_shift`: each row is a permutation.
All inputs are finite; a program needn't handle non-finite values.
Results may differ from a plain program's by a relative error of at most 0.03.
Values may be sent and summed in bfloat16 or wider, within the bound.
A program may use at most 128 MiB of HBM per device.

v0:
```python
import math

import jax
import jax.numpy as jnp
from jax import lax
from jax.sharding import PartitionSpec as P

HQ = 32
KEY_HEADS = 4
HEAD_SIZE = 128
QUERY_PER_KEY = 8


NEGATIVE_FILL = -1e30


def visible(key_pos, query_pos, query_start):
    return (key_pos[None, :] >= query_start[:, None]) & (key_pos[None, :] <= query_pos[:, None])


def over_blocks(carry_state, arrays, advance):
    item_number = arrays[0].shape[0]
    span_length = math.gcd(item_number, 512)
    pieces = item_number // span_length
    stacked = tuple((tensor.reshape((pieces, span_length) + tensor.shape[1:]) for tensor in arrays))

    def scan_step(current, entries):
        return (advance(current, entries), None)

    carry_state, unused = lax.scan(scan_step, carry_state, stacked)
    return carry_state


def on_device(queries, keys, values, output_gradient, doc_lengths, block_order, group_shift):
    groups = lax.axis_size("dp")
    members = lax.axis_size("fsdp")
    group_id = lax.axis_index("dp")
    member = lax.axis_index("fsdp")
    count_of_rows = queries.shape[0]
    block_len = count_of_rows // groups
    rows_per_group = count_of_rows * members
    scaling = 1.0 / math.sqrt(HEAD_SIZE)
    shifts = lax.dynamic_index_in_dim(group_shift, member, 0, keepdims=False)
    send_order = jnp.argsort((group_id + shifts) % groups)

    def outbound(tensor):
        return jnp.take(tensor.reshape(groups, block_len, tensor.shape[1]), send_order, axis=0)

    arrived = (
        lax.all_to_all(outbound(queries), "dp", split_axis=0, concat_axis=0, tiled=True),
        lax.all_to_all(outbound(keys), "dp", split_axis=0, concat_axis=0, tiled=True),
        lax.all_to_all(outbound(values), "dp", split_axis=0, concat_axis=0, tiled=True),
    )
    take_order = (group_id - shifts) % groups

    def settle(tensor):
        return jnp.take(tensor, take_order, axis=0).reshape(count_of_rows, tensor.shape[2])

    rows_of_query = settle(arrived[0])
    key_rows = settle(arrived[1])
    value_rows = settle(arrived[2])
    order_row = lax.dynamic_index_in_dim(block_order, group_id, 0, keepdims=False)
    length_row = lax.dynamic_index_in_dim(doc_lengths, group_id, 0, keepdims=False)
    offsets = jnp.arange(block_len, dtype=jnp.int32)
    slot_pos = (order_row[:, None] * block_len + offsets[None, :]).reshape(rows_per_group)
    doc_ends = jnp.cumsum(length_row)
    slot_start = jnp.sum(
        jnp.where(doc_ends[None, :] <= slot_pos[:, None], length_row[None, :], 0), axis=1
    )
    query_pos = lax.dynamic_slice_in_dim(slot_pos, member * count_of_rows, count_of_rows)
    query_start = lax.dynamic_slice_in_dim(slot_start, member * count_of_rows, count_of_rows)
    query_fourfold = rows_of_query.reshape(count_of_rows, KEY_HEADS, QUERY_PER_KEY, HEAD_SIZE)
    gradient_four = output_gradient.reshape(count_of_rows, KEY_HEADS, QUERY_PER_KEY, HEAD_SIZE)

    def forward_step(carry_state, entries):
        run_max, run_sum, run_acc = carry_state
        key_portion, value_portion, key_pos = entries
        item_number = key_portion.shape[0]
        heads_of_key = key_portion.reshape(item_number, KEY_HEADS, HEAD_SIZE)
        heads_of_value = value_portion.reshape(item_number, KEY_HEADS, HEAD_SIZE)
        scores = (
            jnp.einsum(
                "qcgd,kcd->cgqk", query_fourfold, heads_of_key, preferred_element_type=jnp.float32
            )
            * scaling
        )
        allowed = visible(key_pos, query_pos, query_start)
        scores = jnp.where(allowed, scores, NEGATIVE_FILL)
        new_max = jnp.maximum(run_max, jnp.max(scores, axis=-1))
        weights = jnp.where(allowed, jnp.exp(scores - new_max[..., None]), 0.0)
        factor = jnp.exp(run_max - new_max)
        run_sum = run_sum * factor + jnp.sum(weights, axis=-1)
        update = jnp.einsum(
            "cgqk,kcd->cgqd",
            weights.astype(jnp.bfloat16),
            heads_of_value,
            preferred_element_type=jnp.float32,
        )
        run_acc = run_acc * factor[..., None] + update
        return (new_max, run_sum, run_acc)

    initial = (
        jnp.full((KEY_HEADS, QUERY_PER_KEY, count_of_rows), NEGATIVE_FILL, jnp.float32),
        jnp.zeros((KEY_HEADS, QUERY_PER_KEY, count_of_rows), jnp.float32),
        jnp.zeros((KEY_HEADS, QUERY_PER_KEY, count_of_rows, HEAD_SIZE), jnp.float32),
    )
    piece = (
        lax.all_gather(key_rows, "fsdp", axis=0, tiled=True),
        lax.all_gather(value_rows, "fsdp", axis=0, tiled=True),
    )
    item_number = piece[0].shape[0]
    run_max, run_sum, run_acc = over_blocks(initial, (piece[0], piece[1], slot_pos), forward_step)
    key_everything, value_everything = (
        lax.all_gather(key_rows, "fsdp", axis=0, tiled=True),
        lax.all_gather(value_rows, "fsdp", axis=0, tiled=True),
    )
    attended = (run_acc / run_sum[..., None]).astype(jnp.bfloat16)
    log_total = run_max + jnp.log(run_sum)
    attn_out = attended.transpose(2, 0, 1, 3).reshape(count_of_rows, HQ * HEAD_SIZE)
    row_delta = jnp.sum(
        gradient_four.astype(jnp.float32) * attended.transpose(2, 0, 1, 3).astype(jnp.float32),
        axis=-1,
    ).transpose(1, 2, 0)

    def key_pass(carry_state, entries):
        key_portion, value_portion, key_pos = entries
        item_number = key_portion.shape[0]
        heads_of_key = key_portion.reshape(item_number, KEY_HEADS, HEAD_SIZE)
        heads_of_value = value_portion.reshape(item_number, KEY_HEADS, HEAD_SIZE)
        scores = (
            jnp.einsum(
                "qcgd,kcd->cgqk", query_fourfold, heads_of_key, preferred_element_type=jnp.float32
            )
            * scaling
        )
        allowed = visible(key_pos, query_pos, query_start)
        probs = jnp.where(allowed, jnp.exp(scores - log_total[..., None]), 0.0)
        dprob = jnp.einsum(
            "qcgd,kcd->cgqk", gradient_four, heads_of_value, preferred_element_type=jnp.float32
        )
        dscore = (probs * (dprob - row_delta[..., None])).astype(jnp.bfloat16)
        carry_state = carry_state + jnp.einsum(
            "cgqk,kcd->cgqd", dscore, heads_of_key, preferred_element_type=jnp.float32
        )
        key_gradient = (
            jnp.einsum("cgqk,qcgd->kcd", dscore, query_fourfold, preferred_element_type=jnp.float32)
            * scaling
        )
        value_gradient = jnp.einsum(
            "cgqk,qcgd->kcd",
            probs.astype(jnp.bfloat16),
            gradient_four,
            preferred_element_type=jnp.float32,
        )
        return (
            carry_state,
            (
                key_gradient.reshape(item_number, KEY_HEADS * HEAD_SIZE),
                value_gradient.reshape(item_number, KEY_HEADS * HEAD_SIZE),
            ),
        )

    span_length = math.gcd(rows_per_group, 512)
    block_count = rows_per_group // span_length
    stacked = (
        key_everything.reshape(block_count, span_length, KEY_HEADS * HEAD_SIZE),
        value_everything.reshape(block_count, span_length, KEY_HEADS * HEAD_SIZE),
        slot_pos.reshape(block_count, span_length),
    )
    zeroed_gradient = jnp.zeros((KEY_HEADS, QUERY_PER_KEY, count_of_rows, HEAD_SIZE), jnp.float32)

    def with_terms(carry_state, entries):
        return key_pass(carry_state, entries)

    grad_acc, term_list = lax.scan(with_terms, zeroed_gradient, stacked)
    key_term_list = term_list[0].reshape(rows_per_group, KEY_HEADS * HEAD_SIZE)
    value_term_list = term_list[1].reshape(rows_per_group, KEY_HEADS * HEAD_SIZE)
    own_key, own_value = (
        lax.psum_scatter(
            key_term_list.astype(jnp.bfloat16), "fsdp", scatter_dimension=0, tiled=True
        ).astype(jnp.float32),
        lax.psum_scatter(
            value_term_list.astype(jnp.bfloat16), "fsdp", scatter_dimension=0, tiled=True
        ).astype(jnp.float32),
    )
    grad_q = (
        (grad_acc * scaling)
        .astype(jnp.bfloat16)
        .transpose(2, 0, 1, 3)
        .reshape(count_of_rows, HQ * HEAD_SIZE)
    )
    return (attn_out, grad_q, own_key.astype(jnp.bfloat16), own_value.astype(jnp.bfloat16))


def solution(mesh):
    return jax.shard_map(
        on_device,
        mesh=mesh,
        in_specs=(
            P(("dp", "fsdp"), None),
            P(("dp", "fsdp"), None),
            P(("dp", "fsdp"), None),
            P(("dp", "fsdp"), None),
            P(),
            P(),
            P(),
        ),
        out_specs=(
            P(("dp", "fsdp"), None),
            P(("dp", "fsdp"), None),
            P(("dp", "fsdp"), None),
            P(("dp", "fsdp"), None),
        ),
        check_vma=False,
    )
```

profile of v0, /device:TPU:1, one launch (start us, length us, event | category | flops | bytes accessed | tf_op | source)
XLA Modules:
  0.0 452.7 jit_solution(16416399210071220139)
XLA Ops:
  9.2 1.5 gather_fusion.4
  10.7 1.5 gather_fusion
  12.9 11.6 %all_to_all.15 = bf16[8,16,512]{2,1,0:T(8,128)(2,1)S(1)} all-to-all(bf16[8,16,512]{2,1,0:T(8,128)(2,1)S(1)} %get-tuple-element.357), channel_id=1, replica_groups=mesh['dp'=8,'fsdp'=16] {'dp'}, dimensions={0} | all-to-all | bytes 262144 | tf_op jit(solution)/shard_map/all_to_all | solution.py:52
  24.5 3.4 all-to-all-start
  28.5 4.8 %all-to-all-done = bf16[8,16,512]{2,1,0:T(8,128)(2,1)S(1)} async-done(((bf16[8,16,512]{2,1,0:T(8,128)(2,1)}), bf16[8,16,512]{2,1,0:T(8,128)(2,1)S(1)}, u32[]{:S(2)}, u32[]{:S(2)}) %all-to-all-start) | async-done | bytes 131104 | tf_op jit(solution)/shard_map/all_to_all | solution.py:51
  36.1 1.1 broadcast_select_fusion.1
  37.2 3.6 all-to-all-start.1
  43.2 2.3 copy.82
  45.5 10.7 %all-to-all-done.1 = bf16[8,16,4096]{2,1,0:T(8,128)(2,1)S(1)} async-done(((bf16[8,16,4096]{2,1,0:T(8,128)(2,1)}), bf16[8,16,4096]{2,1,0:T(8,128)(2,1)S(1)}, u32[]{:S(2)}, u32[]{:S(2)}) %all-to-all-start.1) | async-done | bytes 1048608 | tf_op jit(solution)/shard_map/all_to_all | solution.py:50
  58.6 2.0 copy.84
  60.6 29.7 %all-gather.3.cloned.1.call-done = bf16[2048,512]{1,0:T(8,128)(2,1)} async-done(((bf16[128,512]{1,0:T(8,128)(2,1)}), bf16[2048,512]{1,0:T(8,128)(2,1)}) %all-gather.3.cloned.1.call-update) | async-done | bytes 2097168 | tf_op jit(solution)/shard_map/all_gather | solution.py:108
  90.3 4.2 copy.77
  94.5 46.0 %all-gather.5.cloned.1.call-done = bf16[2048,512]{1,0:T(8,128)(2,1)} async-done(((bf16[128,512]{1,0:T(8,128)(2,1)}), bf16[2048,512]{1,0:T(8,128)(2,1)}) %all-gather.5.cloned.1.call-update) | async-done | bytes 2097168 | tf_op jit(solution)/shard_map/all_gather | solution.py:109
  140.4 4.2 copy.79
  144.6 72.3 %while.30 = (s32[]{:T(128)}, f32[4,8,128]{2,1,0:T(8,128)S(1)}, f32[4,8,128]{2,1,0:T(8,128)S(1)}, f32[4,8,128,128]{3,2,1,0:T(8,128)}, s32[4,512]{1,0:T(4,128)S(1)...) while((s32[]{:T(128)}, f32[4,8,128]{2,1,0:T(8,128)S(1)}, ...), condition=%wide.region_6.9_spmd.clone, body=%wide.region_3.8_spmd.clone.sunk | while | flops 1102794752 | bytes 67640488 | solution.py:30
  144.8 2.1 constant_dynamic-slice_fusion.14
  146.8 4.7 %fusion.71 = (f32[4,8,128]{2,1,0:T(8,128)S(1)}, f32[4,512,128,8]{2,1,3,0:T(8,128)}) fusion(pred[128,512]{0,1:T(8,128)(4,1)S(1)} %compare_and_fusion.6, bf16[512,4,128,1]{0,2,3,1:T(8,128)(2,1)S(1)} %bitcast.172, bf16[128,4,8,128]{3,0,2,1:T(8,128)(2,1)S(1)} %get-tuple-element.547), kind=kOutput, calls=%fused_computation.8.clone.1 | convolution fusion | flops 543158272 | bytes 10043392 | tf_op jit(solution)/shard_map/while/body/eval_jaxpr/qcgd,kcd->cgqk/dot_general | solution.py:82
  151.5 4.7 %fusion.72 = f32[4,8,128]{2,1,0:T(8,128)S(1)} fusion(f32[4,512,128,8]{2,1,3,0:T(8,128)} %get-tuple-element.496, f32[4,8,128]{2,1,0:T(8,128)S(1)} %select_maximum_fusion.2, pred[128,512]{0,1:T(8,128)(4,1)S(1)} %compare_and_fusion.6), kind=kLoop, calls=%fused_computation.10.clone.1 | loop fusion | flops 10481664 | bytes 8486912 | tf_op jit(solution)/shard_map/while/body/eval_jaxpr/reduce_sum | solution.py:92
  156.2 1.1 copy-done.1
  157.4 5.1 %fusion.74 = f32[4,8,128,128]{3,2,1,0:T(8,128)} fusion(f32[4,8,128,128]{3,2,1,0:T(8,128)} %get-tuple-element.530, bf16[512,4,128,1]{0,2,3,1:T(8,128)(2,1)} %bitcast.173, f32[4,512,128,8]{2,1,3,0:T(8,128)S(1)} %copy-done.1, f32[4,8,128]{2,1,0:T(8,128)S(1)} %select_maximum_fusion.2, pred[128,512]{0,1:T(8,128)(4,1)S(1)} %compare_and_fusion.6, ...), kind=kOutput, calls=%fused_computation.14.clone.1 | convolution fusion | flops 548929536 | bytes 13205505 | tf_op jit(solution)/shard_map/while/body/eval_jaxpr/cgqk,kcd->cgqd/dot_general | solution.py:93
  162.6 2.1 constant_dynamic-slice_fusion.14
  164.7 4.7 %fusion.71 = (f32[4,8,128]{2,1,0:T(8,128)S(1)}, f32[4,512,128,8]{2,1,3,0:T(8,128)}) fusion(pred[128,512]{0,1:T(8,128)(4,1)S(1)} %compare_and_fusion.6, bf16[512,4,128,1]{0,2,3,1:T(8,128)(2,1)S(1)} %bitcast.172, bf16[128,4,8,128]{3,0,2,1:T(8,128)(2,1)S(1)} %get-tuple-element.547), kind=kOutput, calls=%fused_computation.8.clone.1 | convolution fusion | flops 543158272 | bytes 10043392 | tf_op jit(solution)/shard_map/while/body/eval_jaxpr/qcgd,kcd->cgqk/dot_general | solution.py:82
  169.4 4.7 %fusion.72 = f32[4,8,128]{2,1,0:T(8,128)S(1)} fusion(f32[4,512,128,8]{2,1,3,0:T(8,128)} %get-tuple-element.496, f32[4,8,128]{2,1,0:T(8,128)S(1)} %select_maximum_fusion.2, pred[128,512]{0,1:T(8,128)(4,1)S(1)} %compare_and_fusion.6), kind=kLoop, calls=%fused_computation.10.clone.1 | loop fusion | flops 10481664 | bytes 8486912 | tf_op jit(solution)/shard_map/while/body/eval_jaxpr/reduce_sum | solution.py:92
  174.1 1.1 copy-done.1
  175.2 5.4 %fusion.74 = f32[4,8,128,128]{3,2,1,0:T(8,128)} fusion(f32[4,8,128,128]{3,2,1,0:T(8,128)} %get-tuple-element.530, bf16[512,4,128,1]{0,2,3,1:T(8,128)(2,1)} %bitcast.173, f32[4,512,128,8]{2,1,3,0:T(8,128)S(1)} %copy-done.1, f32[4,8,128]{2,1,0:T(8,128)S(1)} %select_maximum_fusion.2, pred[128,512]{0,1:T(8,128)(4,1)S(1)} %compare_and_fusion.6, ...), kind=kOutput, calls=%fused_computation.14.clone.1 | convolution fusion | flops 548929536 | bytes 13205505 | tf_op jit(solution)/shard_map/while/body/eval_jaxpr/cgqk,kcd->cgqd/dot_general | solution.py:93
  180.8 2.1 constant_dynamic-slice_fusion.14
  182.8 4.7 %fusion.71 = (f32[4,8,128]{2,1,0:T(8,128)S(1)}, f32[4,512,128,8]{2,1,3,0:T(8,128)}) fusion(pred[128,512]{0,1:T(8,128)(4,1)S(1)} %compare_and_fusion.6, bf16[512,4,128,1]{0,2,3,1:T(8,128)(2,1)S(1)} %bitcast.172, bf16[128,4,8,128]{3,0,2,1:T(8,128)(2,1)S(1)} %get-tuple-element.547), kind=kOutput, calls=%fused_computation.8.clone.1 | convolution fusion | flops 543158272 | bytes 10043392 | tf_op jit(solution)/shard_map/while/body/eval_jaxpr/qcgd,kcd->cgqk/dot_general | solution.py:82
  187.5 4.7 %fusion.72 = f32[4,8,128]{2,1,0:T(8,128)S(1)} fusion(f32[4,512,128,8]{2,1,3,0:T(8,128)} %get-tuple-element.496, f32[4,8,128]{2,1,0:T(8,128)S(1)} %select_maximum_fusion.2, pred[128,512]{0,1:T(8,128)(4,1)S(1)} %compare_and_fusion.6), kind=kLoop, calls=%fused_computation.10.clone.1 | loop fusion | flops 10481664 | bytes 8486912 | tf_op jit(solution)/shard_map/while/body/eval_jaxpr/reduce_sum | solution.py:92
  192.2 1.1 copy-done.1
  193.4 5.4 %fusion.74 = f32[4,8,128,128]{3,2,1,0:T(8,128)} fusion(f32[4,8,128,128]{3,2,1,0:T(8,128)} %get-tuple-element.530, bf16[512,4,128,1]{0,2,3,1:T(8,128)(2,1)} %bitcast.173, f32[4,512,128,8]{2,1,3,0:T(8,128)S(1)} %copy-done.1, f32[4,8,128]{2,1,0:T(8,128)S(1)} %select_maximum_fusion.2, pred[128,512]{0,1:T(8,128)(4,1)S(1)} %compare_and_fusion.6, ...), kind=kOutput, calls=%fused_computation.14.clone.1 | convolution fusion | flops 548929536 | bytes 13205505 | tf_op jit(solution)/shard_map/while/body/eval_jaxpr/cgqk,kcd->cgqd/dot_general | solution.py:93
  198.9 2.1 constant_dynamic-slice_fusion.14
  201.0 4.7 %fusion.71 = (f32[4,8,128]{2,1,0:T(8,128)S(1)}, f32[4,512,128,8]{2,1,3,0:T(8,128)}) fusion(pred[128,512]{0,1:T(8,128)(4,1)S(1)} %compare_and_fusion.6, bf16[512,4,128,1]{0,2,3,1:T(8,128)(2,1)S(1)} %bitcast.172, bf16[128,4,8,128]{3,0,2,1:T(8,128)(2,1)S(1)} %get-tuple-element.547), kind=kOutput, calls=%fused_computation.8.clone.1 | convolution fusion | flops 543158272 | bytes 10043392 | tf_op jit(solution)/shard_map/while/body/eval_jaxpr/qcgd,kcd->cgqk/dot_general | solution.py:82
  205.7 4.7 %fusion.72 = f32[4,8,128]{2,1,0:T(8,128)S(1)} fusion(f32[4,512,128,8]{2,1,3,0:T(8,128)} %get-tuple-element.496, f32[4,8,128]{2,1,0:T(8,128)S(1)} %select_maximum_fusion.2, pred[128,512]{0,1:T(8,128)(4,1)S(1)} %compare_and_fusion.6), kind=kLoop, calls=%fused_computation.10.clone.1 | loop fusion | flops 10481664 | bytes 8486912 | tf_op jit(solution)/shard_map/while/body/eval_jaxpr/reduce_sum | solution.py:92
  210.4 1.1 copy-done.1
  211.5 5.4 %fusion.74 = f32[4,8,128,128]{3,2,1,0:T(8,128)} fusion(f32[4,8,128,128]{3,2,1,0:T(8,128)} %get-tuple-element.530, bf16[512,4,128,1]{0,2,3,1:T(8,128)(2,1)} %bitcast.173, f32[4,512,128,8]{2,1,3,0:T(8,128)S(1)} %copy-done.1, f32[4,8,128]{2,1,0:T(8,128)S(1)} %select_maximum_fusion.2, pred[128,512]{0,1:T(8,128)(4,1)S(1)} %compare_and_fusion.6, ...), kind=kOutput, calls=%fused_computation.14.clone.1 | convolution fusion | flops 548929536 | bytes 13205505 | tf_op jit(solution)/shard_map/while/body/eval_jaxpr/cgqk,kcd->cgqd/dot_general | solution.py:93
  217.0 2.9 copy.80
  219.9 3.4 multiply_reduce_fusion
  223.3 76.9 %while.31 = (s32[]{:T(128)}, f32[4,8,128,128]{3,2,1,0:T(8,128)}, bf16[4,512,512]{1,2,0:T(8,128)(2,1)}, bf16[4,512,512]{1,2,0:T(8,128)(2,1)}, s32[4,512]{1,0:T(4,...) while((s32[]{:T(128)}, f32[4,8,128,128]{3,2,1,0:T(8,128)}, ...), condition=%wide.region_9.12_spmd.clone, body=%wide.region_8.11_spmd.clone.sunk | while | flops 2707095552 | bytes 69983936 | solution.py:175
  224.4 1.3 fusion.85
  226.9 4.1 fusion.86
  231.0 1.5 fusion.88
  233.0 3.0 fusion.87
  237.0 5.0 %select_add_fusion.2 = f32[4,8,128,128]{3,2,1,0:T(8,128)} fusion(f32[4,8,128,128]{3,2,1,0:T(8,128)} %get-tuple-element.567, bf16[4,8,128,512]{2,3,1,0:T(8,128)(2,1)} %copy-done.2, bf16[512,4,128,1]{0,2,3,1:T(8,128)(2,1)S(1)} %bitcast.171, pred[]{:T(512)S(6)} %compare.13), kind=kOutput, calls=%fused_computation.35.clone.1 | convolution fusion | flops 537919488 | bytes 8912897 | tf_op jit(solution)/shard_map/while/body/eval_jaxpr/cgqk,kcd->cgqd/dot_general | solution.py:142
  243.1 1.3 fusion.85
  245.7 4.1 fusion.86
  249.8 1.5 fusion.88
  251.7 3.0 fusion.87
  255.7 5.7 %select_add_fusion.2 = f32[4,8,128,128]{3,2,1,0:T(8,128)} fusion(f32[4,8,128,128]{3,2,1,0:T(8,128)} %get-tuple-element.567, bf16[4,8,128,512]{2,3,1,0:T(8,128)(2,1)} %copy-done.2, bf16[512,4,128,1]{0,2,3,1:T(8,128)(2,1)S(1)} %bitcast.171, pred[]{:T(512)S(6)} %compare.13), kind=kOutput, calls=%fused_computation.35.clone.1 | convolution fusion | flops 537919488 | bytes 8912897 | tf_op jit(solution)/shard_map/while/body/eval_jaxpr/cgqk,kcd->cgqd/dot_general | solution.py:142
  262.5 1.3 fusion.85
  265.1 4.1 fusion.86
  269.2 1.5 fusion.88
  271.1 3.0 fusion.87
  275.1 5.7 %select_add_fusion.2 = f32[4,8,128,128]{3,2,1,0:T(8,128)} fusion(f32[4,8,128,128]{3,2,1,0:T(8,128)} %get-tuple-element.567, bf16[4,8,128,512]{2,3,1,0:T(8,128)(2,1)} %copy-done.2, bf16[512,4,128,1]{0,2,3,1:T(8,128)(2,1)S(1)} %bitcast.171, pred[]{:T(512)S(6)} %compare.13), kind=kOutput, calls=%fused_computation.35.clone.1 | convolution fusion | flops 537919488 | bytes 8912897 | tf_op jit(solution)/shard_map/while/body/eval_jaxpr/cgqk,kcd->cgqd/dot_general | solution.py:142
  281.9 1.3 fusion.85
  284.5 4.1 fusion.86
  288.6 1.5 fusion.88
  290.5 3.0 fusion.87
  294.5 5.7 %select_add_fusion.2 = f32[4,8,128,128]{3,2,1,0:T(8,128)} fusion(f32[4,8,128,128]{3,2,1,0:T(8,128)} %get-tuple-element.567, bf16[4,8,128,512]{2,3,1,0:T(8,128)(2,1)} %copy-done.2, bf16[512,4,128,1]{0,2,3,1:T(8,128)(2,1)S(1)} %bitcast.171, pred[]{:T(512)S(6)} %compare.13), kind=kOutput, calls=%fused_computation.35.clone.1 | convolution fusion | flops 537919488 | bytes 8912897 | tf_op jit(solution)/shard_map/while/body/eval_jaxpr/cgqk,kcd->cgqd/dot_general | solution.py:142
  300.3 4.1 copy.87
  304.5 4.3 copy.88
  309.8 1.4 copy.116
  311.2 1.3 copy.102
  312.5 59.3 %reduce-scatter.3.cloned.1.call-done = bf16[128,512]{1,0:T(8,128)(2,1)} async-done(((bf16[2048,512]{1,0:T(8,128)(2,1)}), bf16[128,512]{1,0:T(8,128)(2,1)}) %reduce-scatter.3.cloned.1.call-update) | async-done | bytes 131088 | tf_op jit(solution)/shard_map/reduce_scatter | solution.py:179
  371.8 74.3 %reduce-scatter.5.cloned.1.call-done = bf16[128,512]{1,0:T(8,128)(2,1)} async-done(((bf16[2048,512]{1,0:T(8,128)(2,1)}), bf16[128,512]{1,0:T(8,128)(2,1)}) %reduce-scatter.5.cloned.1.call-update) | async-done | bytes 131088 | tf_op jit(solution)/shard_map/reduce_scatter | solution.py:182
  (109 shorter events, 27.8 us)
Async XLA Ops:
  7.2 28.3 %copy-start = (bf16[128,4096]{1,0:T(8,128)(2,1)S(1)}, bf16[128,4096]{1,0:T(8,128)(2,1)}, u32[]{:S(2)}) copy-start(bf16[128,4096]{1,0:T(8,128)(2,1)} %param.15) | copy-start | bytes 3145732
  24.5 8.8 %all-to-all-start = ((bf16[8,16,512]{2,1,0:T(8,128)(2,1)}), bf16[8,16,512]{2,1,0:T(8,128)(2,1)S(1)}, u32[]{:S(2)}, u32[]{:S(2)}) async-start(bf16[8,16,512]{2,1,0:T(8,128)(2,1)} %get-tuple-element.358), calls=%async_computation | async-start | bytes 262144 | tf_op jit(solution)/shard_map/all_to_all | solution.py:51
  27.9 62.4 %all-gather.3.cloned.1.call-start = ((), (), s32[]{:S(2)}) async-start(), calls=%async_computation.5 | async-start | bytes 2228224 | tf_op jit(solution)/shard_map/all_gather | solution.py:108
  34.7 105.8 %all-gather.5.cloned.1.call-start = ((), (), s32[]{:S(2)}) async-start(), calls=%async_computation.6 | async-start | bytes 2228224 | tf_op jit(solution)/shard_map/all_gather | solution.py:109
  37.2 19.0 %all-to-all-start.1 = ((bf16[8,16,4096]{2,1,0:T(8,128)(2,1)}), bf16[8,16,4096]{2,1,0:T(8,128)(2,1)S(1)}, u32[]{:S(2)}, u32[]{:S(2)}) async-start(bf16[8,16,4096]{2,1,0:T(8,128)(2,1)} %broadcast_select_fusion.1), calls=%async_computation.1 | async-start | bytes 2097152 | tf_op jit(solution)/shard_map/all_to_all | solution.py:50
  40.8 331.1 %reduce-scatter.3.cloned.1.call-start = ((), (), s32[]{:S(2)}) async-start(), calls=%async_computation.7 | async-start | bytes 2228224 | tf_op jit(solution)/shard_map/reduce_scatter | solution.py:179
  57.2 1.0 copy-start.4
  151.5 5.8 %copy-start.1 = (f32[4,512,128,8]{2,1,3,0:T(8,128)S(1)}, f32[4,512,128,8]{2,1,3,0:T(8,128)}, u32[]{:S(2)}) copy-start(f32[4,512,128,8]{2,1,3,0:T(8,128)} %get-tuple-element.496) | copy-start | bytes 25165828 | tf_op jit(solution)/shard_map/while
  169.4 5.8 %copy-start.1 = (f32[4,512,128,8]{2,1,3,0:T(8,128)S(1)}, f32[4,512,128,8]{2,1,3,0:T(8,128)}, u32[]{:S(2)}) copy-start(f32[4,512,128,8]{2,1,3,0:T(8,128)} %get-tuple-element.496) | copy-start | bytes 25165828 | tf_op jit(solution)/shard_map/while
  187.5 5.8 %copy-start.1 = (f32[4,512,128,8]{2,1,3,0:T(8,128)S(1)}, f32[4,512,128,8]{2,1,3,0:T(8,128)}, u32[]{:S(2)}) copy-start(f32[4,512,128,8]{2,1,3,0:T(8,128)} %get-tuple-element.496) | copy-start | bytes 25165828 | tf_op jit(solution)/shard_map/while
  205.7 5.8 %copy-start.1 = (f32[4,512,128,8]{2,1,3,0:T(8,128)S(1)}, f32[4,512,128,8]{2,1,3,0:T(8,128)}, u32[]{:S(2)}) copy-start(f32[4,512,128,8]{2,1,3,0:T(8,128)} %get-tuple-element.496) | copy-start | bytes 25165828 | tf_op jit(solution)/shard_map/while
  231.0 1.9 copy-start.2
  249.8 1.9 copy-start.2
  269.2 1.9 copy-start.2
  288.6 1.9 copy-start.2
  304.4 4.4 copy-start.3
  304.4 141.7 %reduce-scatter.5.cloned.1.call-start = ((), (), s32[]{:S(2)}) async-start(), calls=%async_computation.8 | async-start | bytes 2228224 | tf_op jit(solution)/shard_map/reduce_scatter | solution.py:182
  309.1 2.1 copy-start.5
Sparse Core Ops, SparseCore 0:
  34.8 55.4 all-gather.2
  93.3 47.0 all-gather.4
  304.6 67.2 reduce-scatter.2
  376.2 69.8 reduce-scatter.4
where the time goes:
time: 455 us; the launch traced here: 453 us
  waiting for transfers between devices  226 us (50%)
  matrix products  102 us (22%)
  local copies, waits for them, and re-layouts  63 us (14%)
  other arithmetic  29.5 us (6%)
  between operations  14 us (3%)
  blocking collectives  11.6 us (3%)
  starting transfers between devices  7.1 us (2%)
    reduce_scatter x1, waiting for transfers between devices, on_device(): lax.psum_scatter(value_term_list.astype(jnp.bfloat16), 'fsdp', scatter_di...  74.3 us
    reduce_scatter x1, waiting for transfers between devices, on_device(): lax.psum_scatter(key_term_list.astype(jnp.bfloat16), 'fsdp', scatter_dime...  59.3 us
    all_gather x1, waiting for transfers between devices, on_device(): lax.all_gather(value_rows, 'fsdp', axis=0, tiled=True)  46 us
    all_gather x1, waiting for transfers between devices, on_device(): lax.all_gather(key_rows, 'fsdp', axis=0, tiled=True)  29.7 us
    dot_general x4, matrix products, key_pass(): jnp.einsum('cgqk,kcd->cgqd', dscore, heads_of_key, preferred_element_type...  22.2 us
    dot_general x4, matrix products, forward_step(): jnp.einsum('cgqk,kcd->cgqd', weights.astype(jnp.bfloat16), heads_of_value...  21.4 us
    dot_general x4, matrix products, forward_step(): jnp.einsum('qcgd,kcd->cgqk', query_fourfold, heads_of_key, preferred_elem...  18.7 us
    reduce_sum x4, other arithmetic, forward_step(): run_sum = run_sum * factor + jnp.sum(weights, axis=-1)  18.7 us
  transfers between devices with their start and end apart: 6, of which 6 were waited for; matrix products, arithmetic and copies ran while one was open for 5% of the time, Pallas kernels for 0%

commit v1 on v0

v1 whole, which is shorter than its diff:
```python
import functools
import math

import jax
import jax.numpy as jnp
from jax import lax
from jax.experimental import pallas as pl
from jax.experimental.pallas import tpu as pltpu
from jax.sharding import PartitionSpec as P

HEADS = 32
KEY_HEADS = 4
HEAD = 128
PER_KEY = 8
BLOCK = 16
ROWS = 128
GROUPS = 8
MEMBERS = 16
CHIPS = 8
GROUP_ROWS = 2048
HALF = HEADS * HEAD // 2
KEYS_HALF = KEY_HEADS * HEAD // 2
CHUNK = 128
MOST_CHUNKS = 9
SCALE = 1.0 / math.sqrt(HEAD)
LOG2E = 1.4426950408889634
FILL = -1e30
MESH = pl.DeviceIdType.MESH
MIB = 1 << 20


def place():
    group = lax.axis_index("dp")
    member = lax.axis_index("fsdp")
    return group, member // 8, (member // 2) % 4, member % 2


def member_of(zh, x, core):
    return zh * 8 + x * 2 + core


def gather_kernel(
    q_ref, k_ref, v_ref, do_ref, shift_ref, order_ref,
    rq_ref, do2_ref, kv_ref, table_ref,
    send_q, send_kv, q_ssem, q_rsem, kv_ssem, kv_rsem, do_ssem, do_rsem, g_ssem, g_rsem, local_sem,
):
    group, zh, x, core = place()
    member = member_of(zh, x, core)
    chip = zh * 4 + x
    right, left = (x + 1) % 4, (x + 3) % 4
    other = 1 - core
    z_peer = (group, member_of(1 - zh, x, core))
    r_peer = (group, member_of(zh, right, core))
    l_peer = (group, member_of(zh, left, core))
    core_peer = (group, member_of(zh, x, other))

    barrier = pltpu.get_barrier_semaphore()
    greeted = 0
    for dev in (z_peer, r_peer, l_peer, core_peer):
        pl.semaphore_signal(barrier, inc=1, device_id=dev, device_id_type=MESH)
        greeted += 1
    for step in range(1, GROUPS):
        for side in range(2):
            dev = ((group + GROUPS - step) % GROUPS, member_of(zh, x, side))
            pl.semaphore_signal(barrier, inc=1, device_id=dev, device_id_type=MESH)
            greeted += 1

    def block_for(row, step):
        found = jnp.int32(0)
        for b in range(GROUPS):
            found = jnp.maximum(found, jnp.where(shift_ref[row, b] == step, b, 0))
        return found

    for step in range(GROUPS):
        b = block_for(member, step)
        for side in range(2):
            cols = slice(side * KEYS_HALF, (side + 1) * KEYS_HALF)
            send_kv[step, side, :, 0:KEYS_HALF] = k_ref[b, :, cols]
            send_kv[step, side, :, KEYS_HALF:] = v_ref[b, :, cols]

    pl.semaphore_wait(barrier, greeted)

    def kv_copy(step, flip):
        side = core if flip == 0 else other
        return pltpu.make_async_remote_copy(
            src_ref=send_kv.at[step, side],
            dst_ref=kv_ref.at[chip, core, step],
            send_sem=kv_ssem.at[step, flip],
            recv_sem=kv_rsem.at[step, flip],
            device_id=((group + step) % GROUPS, member_of(zh, x, side)),
            device_id_type=MESH,
        )

    own_kv = pltpu.make_async_copy(send_kv.at[0, core], kv_ref.at[chip, core, 0], local_sem.at[0])
    own_kv.start()
    kv_copies = [kv_copy(s, f) for s in range(GROUPS) for f in range(2) if s or f]
    for copy in kv_copies:
        copy.start()

    for step in range(GROUPS):
        send_q[step] = q_ref[block_for(member, step)]

    def halves(ref, side):
        return ref.at[:, pl.ds(pl.multiple_of(side * HALF, HALF), HALF)]

    def do_peer():
        return pltpu.make_async_remote_copy(
            src_ref=halves(do_ref, other),
            dst_ref=do2_ref.at[core],
            send_sem=do_ssem,
            recv_sem=do_rsem,
            device_id=core_peer,
            device_id_type=MESH,
        )

    do_copy = do_peer()
    do_copy.start()
    own_do = pltpu.make_async_copy(halves(do_ref, core), do2_ref.at[core], local_sem.at[1])
    own_do.start()

    for copy in kv_copies:
        copy.wait()
    own_kv.wait()

    def send_region(index, src, dev):
        return pltpu.make_async_remote_copy(
            src_ref=src,
            dst_ref=src,
            send_sem=g_ssem.at[index],
            recv_sem=g_rsem.at[index],
            device_id=dev,
            device_id_type=MESH,
        )

    chip_z = (1 - zh) * 4 + x
    own_z = send_region(0, kv_ref.at[chip], z_peer)
    own_r = send_region(1, kv_ref.at[chip], r_peer)
    own_l = send_region(2, kv_ref.at[chip], l_peer)
    own_z.start()
    own_r.start()
    own_l.start()

    def q_copy(step, flip):
        side = core if flip == 0 else other
        return pltpu.make_async_remote_copy(
            src_ref=send_q.at[step, :, pl.ds(pl.multiple_of(side * HALF, HALF), HALF)],
            dst_ref=rq_ref.at[core, step],
            send_sem=q_ssem.at[step, flip],
            recv_sem=q_rsem.at[step, flip],
            device_id=((group + step) % GROUPS, member_of(zh, x, side)),
            device_id_type=MESH,
        )

    own_q = pltpu.make_async_copy(
        send_q.at[0, :, pl.ds(pl.multiple_of(core * HALF, HALF), HALF)], rq_ref.at[core, 0], local_sem.at[2]
    )
    own_q.start()
    q_copies = [q_copy(s, f) for s in range(GROUPS) for f in range(2) if s or f]
    for copy in q_copies:
        copy.start()

    def fill(row, carry):
        for step in range(GROUPS):
            b = block_for(row, step)
            table_ref[row * GROUPS + step] = order_ref[group, row * GROUPS + b]
        return carry

    lax.fori_loop(0, MEMBERS, fill, 0)
    for side in range(2):
        row = member_of(zh, x, side)
        for step in range(GROUPS):
            b = block_for(row, step)
            table_ref[128 + side * GROUPS + step] = order_ref[group, row * GROUPS + b]
            table_ref[144 + side * GROUPS + step] = b

    own_z.wait_recv()
    z_r = send_region(3, kv_ref.at[chip_z], r_peer)
    z_l = send_region(4, kv_ref.at[chip_z], l_peer)
    z_r.start()
    z_l.start()
    own_r.wait_recv()
    far_r = send_region(5, kv_ref.at[zh * 4 + left, 0], r_peer)
    far_r.start()
    own_l.wait_recv()
    far_l = send_region(6, kv_ref.at[zh * 4 + right, 1], l_peer)
    far_l.start()
    z_r.wait_recv()
    zfar_r = send_region(7, kv_ref.at[(1 - zh) * 4 + left, 0], r_peer)
    zfar_r.start()
    z_l.wait_recv()
    zfar_l = send_region(8, kv_ref.at[(1 - zh) * 4 + right, 1], l_peer)
    zfar_l.start()
    for copy in (far_r, far_l, zfar_r, zfar_l):
        copy.wait_recv()
    for copy in (own_z, own_r, own_l, z_r, z_l, far_r, far_l, zfar_r, zfar_l):
        copy.wait_send()
    for copy in q_copies:
        copy.wait()
    do_copy.wait()
    own_do.wait()
    own_q.wait()


def attend_kernel(
    table_ref, lengths_ref, order_ref, rq_ref, do_ref, kv_ref,
    attn_ref, dq_ref, dkv_ref,
    ks, acc, turned, sem,
):
    group = lax.axis_index("dp")

    def arrange(slot, carry):
        dst = pl.multiple_of(table_ref[slot] * BLOCK, BLOCK)
        pltpu.make_async_copy(kv_ref.at[slot], ks.at[pl.ds(dst, BLOCK)], sem).start()
        return carry

    lax.fori_loop(0, MEMBERS * GROUPS, arrange, 0)
    acc[...] = jnp.zeros_like(acc)
    pltpu.make_async_copy(ks, ks, sem).wait()

    def item(index, carry):
        p = table_ref[128 + index]
        out_row = pl.multiple_of((index // GROUPS) * ROWS + table_ref[144 + index] * BLOCK, BLOCK)
        in_row = pl.multiple_of(index * BLOCK, BLOCK)
        pos = p * BLOCK + lax.broadcasted_iota(jnp.int32, (BLOCK, CHUNK), 0)
        start = jnp.zeros((BLOCK, CHUNK), jnp.int32)
        first = jnp.int32(0)
        end = jnp.int32(0)
        for e in range(8):
            length = lengths_ref[group, e]
            end = end + length
            start = start + jnp.where(end <= pos, length, 0)
            first = first + jnp.where(end <= p * BLOCK, length, 0)
        low = first // CHUNK
        count = (p * BLOCK + BLOCK - 1) // CHUNK - low + 1
        base = pl.multiple_of(low * CHUNK, CHUNK)

        def run(n):
            width = n * CHUNK
            lanes = lax.broadcasted_iota(jnp.int32, (BLOCK, CHUNK), 1)
            parts = []
            for c in range(n):
                key = base + c * CHUNK + lanes
                parts.append(jnp.where((key >= start) & (key <= pos), 0.0, FILL).astype(jnp.float32))
            bias = jnp.concatenate(parts, axis=1) if n > 1 else parts[0]
            keys = pl.ds(base, width)
            for h in range(2):
                def heads(ref, row):
                    return jnp.concatenate(
                        [ref[pl.ds(row, BLOCK), pl.ds((h * PER_KEY + g) * HEAD, HEAD)] for g in range(PER_KEY)], axis=0
                    )

                q = heads(rq_ref, in_row)
                do = heads(do_ref, out_row)
                k = ks[keys, pl.ds(h * HEAD, HEAD)]
                v = ks[keys, pl.ds(KEYS_HALF + h * HEAD, HEAD)]
                s = lax.dot_general(q, k, (((1,), (1,)), ((), ())), preferred_element_type=jnp.float32)
                s = (s.reshape(PER_KEY, BLOCK, width) + bias[None]).reshape(PER_KEY * BLOCK, width)
                dp = lax.dot_general(do, v, (((1,), (1,)), ((), ())), preferred_element_type=jnp.float32)
                top = jnp.max(s, axis=1, keepdims=True)
                w = jnp.exp2((s - top) * (SCALE * LOG2E))
                total = jnp.sum(w, axis=1, keepdims=True)
                w_low = w.astype(jnp.bfloat16)
                inv = 1.0 / total
                out = lax.dot_general(w_low, v, (((1,), (0,)), ((), ())), preferred_element_type=jnp.float32)
                out = (out * inv).astype(jnp.bfloat16)
                do_wide = do.astype(jnp.float32)
                delta = jnp.sum(do_wide * out.astype(jnp.float32), axis=1, keepdims=True)
                ds = (w * (dp - delta)).astype(jnp.bfloat16)
                gq = lax.dot_general(ds, k, (((1,), (0,)), ((), ())), preferred_element_type=jnp.float32)
                gq = (gq * (inv * SCALE)).astype(jnp.bfloat16)
                qs = (q.astype(jnp.float32) * (inv * SCALE)).astype(jnp.bfloat16)
                dos = (do_wide * inv).astype(jnp.bfloat16)
                acc[h, 0, :, keys] += lax.dot_general(
                    qs, ds, (((0,), (0,)), ((), ())), preferred_element_type=jnp.float32
                )
                acc[h, 1, :, keys] += lax.dot_general(
                    dos, w_low, (((0,), (0,)), ((), ())), preferred_element_type=jnp.float32
                )
                for g in range(PER_KEY):
                    cols = pl.ds((h * PER_KEY + g) * HEAD, HEAD)
                    attn_ref[pl.ds(out_row, BLOCK), cols] = out[g * BLOCK:(g + 1) * BLOCK]
                    dq_ref[pl.ds(out_row, BLOCK), cols] = gq[g * BLOCK:(g + 1) * BLOCK]

        for n in range(1, MOST_CHUNKS + 1):
            pl.when(count == n)(functools.partial(run, n))
        return carry

    lax.fori_loop(0, 2 * GROUPS, item, 0)

    def turn(c, carry):
        keys = pl.ds(pl.multiple_of(c * CHUNK, CHUNK), CHUNK)
        for h in range(2):
            for which in range(2):
                turned[keys, pl.ds(which * KEYS_HALF + h * HEAD, HEAD)] = acc[h, which, :, keys].T.astype(jnp.bfloat16)
        return carry

    lax.fori_loop(0, GROUP_ROWS // CHUNK, turn, 0)

    def restore(slot, carry):
        src = pl.multiple_of(order_ref[group, slot] * BLOCK, BLOCK)
        pltpu.make_async_copy(turned.at[pl.ds(src, BLOCK)], dkv_ref.at[slot], sem).start()
        return carry

    lax.fori_loop(0, MEMBERS * GROUPS, restore, 0)
    pltpu.make_async_copy(dkv_ref, dkv_ref, sem).wait()


def scatter_kernel(
    attn2_ref, dq2_ref, u_ref,
    attn_ref, dq_ref, gk_ref, gv_ref,
    far_in, near_out, near_in, z_in, core_in, z_out, total, o_ssem, o_rsem, f_ssem, f_rsem, n_ssem, n_rsem, z_ssem, z_rsem, local_sem,
):
    group, zh, x, core = place()
    right, left, across = (x + 1) % 4, (x + 3) % 4, (x + 2) % 4
    other = 1 - core
    z_peer = (group, member_of(1 - zh, x, core))
    r_peer = (group, member_of(zh, right, core))
    l_peer = (group, member_of(zh, left, core))
    core_peer = (group, member_of(zh, x, other))
    barrier = pltpu.get_barrier_semaphore()
    for dev in (z_peer, r_peer, l_peer, core_peer):
        pl.semaphore_signal(barrier, inc=1, device_id=dev, device_id_type=MESH)
    pl.semaphore_wait(barrier, 4)

    def remote(src, dst, ssem, rsem, dev):
        return pltpu.make_async_remote_copy(
            src_ref=src, dst_ref=dst, send_sem=ssem, recv_sem=rsem, device_id=dev, device_id_type=MESH
        )

    planes = (1 - zh, zh)
    far = {}
    near = {}
    for p in range(2):
        for d, dev in ((0, r_peer), (1, l_peer)):
            far[p, d] = remote(
                u_ref.at[planes[p] * 4 + across, d], far_in.at[d, p], f_ssem.at[d, p], f_rsem.at[d, p], dev
            )
            far[p, d].start()
    for p in range(2):
        for d, dev, to in ((0, r_peer, right), (1, l_peer, left)):
            near[p, d, 1] = remote(
                u_ref.at[planes[p] * 4 + to, 1 - d], near_in.at[d, p, 1 - d], n_ssem.at[d, p, 1], n_rsem.at[d, p, 1], dev
            )
            near[p, d, 1].start()

    cols = pl.ds(pl.multiple_of(core * HALF, HALF), HALF)
    out_copies = []
    for i, (src, dst) in enumerate(((attn2_ref, attn_ref), (dq2_ref, dq_ref))):
        copy = remote(src.at[other], dst.at[:, cols], o_ssem.at[i], o_rsem.at[i], core_peer)
        copy.start()
        out_copies.append(copy)
        copy = pltpu.make_async_copy(src.at[core], dst.at[:, cols], local_sem.at[i])
        copy.start()
        out_copies.append(copy)

    for p in range(2):
        for d, dev, to in ((0, r_peer, right), (1, l_peer, left)):
            far[p, d].wait_recv()
            near_out[d, p] = (
                u_ref[planes[p] * 4 + to, d].astype(jnp.float32) + far_in[d, p].astype(jnp.float32)
            ).astype(jnp.bfloat16)
            near[p, d, 0] = remote(near_out.at[d, p], near_in.at[d, p, d], n_ssem.at[d, p, 0], n_rsem.at[d, p, 0], dev)
            near[p, d, 0].start()

    def summed(p):
        for d in range(2):
            for piece in range(2):
                near[p, d, piece].wait_recv()
        return (
            u_ref[planes[p] * 4 + x].astype(jnp.float32)
            + near_in[0, p].astype(jnp.float32)
            + near_in[1, p].astype(jnp.float32)
        )

    z_out[...] = summed(0).astype(jnp.bfloat16)
    z_copy = remote(z_out, z_in, z_ssem.at[0], z_rsem.at[0], z_peer)
    z_copy.start()
    mine = summed(1)
    z_copy.wait_recv()
    total[...] = (mine + z_in[...].astype(jnp.float32)).astype(jnp.bfloat16)
    core_copy = remote(total.at[other], core_in, z_ssem.at[1], z_rsem.at[1], core_peer)
    core_copy.start()
    here = pl.ds(pl.multiple_of(core * KEYS_HALF, KEYS_HALF), KEYS_HALF)
    there = pl.ds(pl.multiple_of(other * KEYS_HALF, KEYS_HALF), KEYS_HALF)
    gk_ref[:, here] = total[core, :, 0:KEYS_HALF]
    gv_ref[:, here] = total[core, :, KEYS_HALF:]
    core_copy.wait_recv()
    gk_ref[:, there] = core_in[:, 0:KEYS_HALF]
    gv_ref[:, there] = core_in[:, KEYS_HALF:]
    z_copy.wait_send()
    core_copy.wait_send()
    for copy in list(far.values()) + list(near.values()):
        copy.wait_send()
    for copy in out_copies:
        copy.wait()


VMEM = pl.BlockSpec(memory_space=pltpu.VMEM)
SMEM = pl.BlockSpec(memory_space=pltpu.SMEM)
ANY = pl.BlockSpec(memory_space=pl.ANY)


def on_device(queries, keys, values, output_gradient, doc_lengths, block_order, group_shift):
    low = jnp.bfloat16
    dma = pltpu.SemaphoreType.DMA
    rq, do2, kv, table = pl.pallas_call(
        gather_kernel,
        out_shape=(
            jax.ShapeDtypeStruct((2, GROUPS, BLOCK, HALF), low),
            jax.ShapeDtypeStruct((2, ROWS, HALF), low),
            jax.ShapeDtypeStruct((CHIPS, 2, GROUPS, BLOCK, 2 * KEYS_HALF), low),
            jax.ShapeDtypeStruct((256,), jnp.int32),
        ),
        in_specs=[VMEM, VMEM, VMEM, ANY, SMEM, SMEM],
        out_specs=(ANY, ANY, ANY, SMEM),
        scratch_shapes=[
            pltpu.VMEM((GROUPS, BLOCK, 2 * HALF), low),
            pltpu.VMEM((GROUPS, 2, BLOCK, 2 * KEYS_HALF), low),
            dma((GROUPS, 2)), dma((GROUPS, 2)),
            dma((GROUPS, 2)), dma((GROUPS, 2)),
            dma, dma,
            dma((9,)), dma((9,)),
            dma((3,)),
        ],
        compiler_params=pltpu.CompilerParams(collective_id=1, has_side_effects=True, vmem_limit_bytes=16 * MIB),
        name="move_and_gather",
    )(
        queries.reshape(GROUPS, BLOCK, 2 * HALF), keys.reshape(GROUPS, BLOCK, 2 * KEYS_HALF),
        values.reshape(GROUPS, BLOCK, 2 * KEYS_HALF), output_gradient, group_shift, block_order,
    )

    attn2, dq2, dkv = pl.pallas_call(
        attend_kernel,
        out_shape=(
            jax.ShapeDtypeStruct((2 * ROWS, HALF), low),
            jax.ShapeDtypeStruct((2 * ROWS, HALF), low),
            jax.ShapeDtypeStruct((MEMBERS * GROUPS, BLOCK, 2 * KEYS_HALF), low),
        ),
        in_specs=[SMEM, SMEM, SMEM, VMEM, VMEM, ANY],
        out_specs=(VMEM, VMEM, ANY),
        scratch_shapes=[
            pltpu.VMEM((GROUP_ROWS, 2 * KEYS_HALF), low),
            pltpu.VMEM((2, 2, HEAD, GROUP_ROWS), jnp.float32),
            pltpu.VMEM((GROUP_ROWS, 2 * KEYS_HALF), low),
            dma,
        ],
        compiler_params=pltpu.CompilerParams(vmem_limit_bytes=48 * MIB),
        name="attend",
    )(
        table, doc_lengths, block_order,
        rq.reshape(2 * ROWS, HALF), do2.reshape(2 * ROWS, HALF),
        kv.reshape(MEMBERS * GROUPS, BLOCK, 2 * KEYS_HALF),
    )

    return pl.pallas_call(
        scatter_kernel,
        out_shape=(
            jax.ShapeDtypeStruct((ROWS, 2 * HALF), low),
            jax.ShapeDtypeStruct((ROWS, 2 * HALF), low),
            jax.ShapeDtypeStruct((ROWS, 2 * KEYS_HALF), low),
            jax.ShapeDtypeStruct((ROWS, 2 * KEYS_HALF), low),
        ),
        in_specs=[ANY, ANY, VMEM],
        out_specs=(ANY, ANY, VMEM, VMEM),
        scratch_shapes=[
            pltpu.VMEM((2, 2, ROWS, 2 * KEYS_HALF), low),
            pltpu.VMEM((2, 2, ROWS, 2 * KEYS_HALF), low),
            pltpu.VMEM((2, 2, 2, ROWS, 2 * KEYS_HALF), low),
            pltpu.VMEM((2, ROWS, 2 * KEYS_HALF), low),
            pltpu.VMEM((ROWS, 2 * KEYS_HALF), low),
            pltpu.VMEM((2, ROWS, 2 * KEYS_HALF), low),
            pltpu.VMEM((2, ROWS, 2 * KEYS_HALF), low),
            dma((2,)), dma((2,)),
            dma((2, 2)), dma((2, 2)),
            dma((2, 2, 2)), dma((2, 2, 2)),
            dma((2,)), dma((2,)),
            dma((2,)),
        ],
        compiler_params=pltpu.CompilerParams(collective_id=2, has_side_effects=True, vmem_limit_bytes=32 * MIB),
        name="reduce_and_share",
    )(attn2.reshape(2, ROWS, HALF), dq2.reshape(2, ROWS, HALF), dkv.reshape(CHIPS, 2, ROWS, 2 * KEYS_HALF))


def solution(mesh):
    rows = P(("dp", "fsdp"), None)
    return jax.shard_map(
        on_device,
        mesh=mesh,
        in_specs=(rows, rows, rows, rows, P(), P(), P()),
        out_specs=(rows, rows, rows, rows),
        check_vma=False,
    )
```

time: 455 us -> 114 us (0.25)
  waiting for transfers between devices: 226 us -> 0 us
  matrix products: 102 us -> 0 us
  Pallas kernels: 0 us -> 101 us
  local copies, waits for them, and re-layouts: 63 us -> 11.9 us
  other arithmetic: 29.5 us -> 0 us
  between operations: 14 us -> 0.7 us
  blocking collectives: 11.6 us -> 0 us
  starting transfers between devices: 7.1 us -> 0 us
    reduce_scatter x2 -> x0, waiting for transfers between devices: 134 us -> none  [the longest x1 74.3 us: on_device(): lax.psum_scatter(value_term_list.astype(jnp.bfloat16), 'fsdp', scatter_di...]
    dot_general x28 -> x0, matrix products: 102 us -> none  [the longest x4 22.2 us: key_pass(): jnp.einsum('cgqk,kcd->cgqd', dscore, heads_of_key, preferred_element_type...]
    pallas_call x0 -> x3, Pallas kernels: none -> 101 us  [the longest x1 44.2 us: on_device(): pl.pallas_call(gather_kernel, out_shape=(jax.ShapeDtypeStruct((2, GROUPS,...]
    all_gather x2 -> x0, waiting for transfers between devices: 75.7 us -> none  [the longest x1 46 us: on_device(): lax.all_gather(value_rows, 'fsdp', axis=0, tiled=True)]
    reduce_sum x6 -> x0, other arithmetic: 22.2 us -> none  [the longest x4 18.7 us: forward_step(): run_sum = run_sum * factor + jnp.sum(weights, axis=-1)]
    dynamic_slice x22 -> x0, local copies, waits for them, and re-layouts: 17.1 us -> none  [the longest x20 17 us: over_blocks(): carry_state, unused = lax.scan(scan_step, carry_state, stacked)]
    all_to_all x2 -> x0, waiting for transfers between devices: 15.5 us -> none  [the longest x1 10.7 us: on_device(): lax.all_to_all(outbound(queries), 'dp', split_axis=0, concat_axis=0, tile...]
    all_to_all x1 -> x0, blocking collectives: 11.6 us -> none  [on_device(): lax.all_to_all(outbound(values), 'dp', split_axis=0, concat_axis=0, tiled...]
  transfers between devices with their start and end apart: 6 -> 0, of which waited for: 6 -> 0; matrix products, arithmetic and copies ran while one was open for 5% -> 0% of each run, Pallas kernels for 0% -> 0%
where the time goes in v1:
time: 114 us; the launch traced here: 113 us
  Pallas kernels  101 us (89%)
  local copies, waits for them, and re-layouts  11.9 us (10%)
    pallas_call x1, Pallas kernels, on_device(): pl.pallas_call(gather_kernel, out_shape=(jax.ShapeDtypeStruct((2, GROUPS,...  44.2 us
    pallas_call x1, Pallas kernels, on_device(): pl.pallas_call(scatter_kernel, out_shape=(jax.ShapeDtypeStruct((ROWS, 2 *...  28.7 us
    pallas_call x1, Pallas kernels, on_device(): pl.pallas_call(attend_kernel, out_shape=(jax.ShapeDtypeStruct((2 * ROWS,...  27.7 us
    unnamed x23, local copies, waits for them, and re-layouts  11.9 us

profile of v1, /device:TPU:1, one launch (start us, length us, event | category | flops | bytes accessed | tf_op | source)
XLA Modules:
  0.0 113.2 jit_solution(14144178891787013598)
XLA Ops:
  0.6 0.0 copy-start.7
  0.6 0.0 copy-start.8
  0.7 0.8 copy.11.shift_ref
  1.4 0.0 copy-start.2
  1.4 1.2 %copy-done.2 = bf16[128,4096]{1,0:T(8,128)(2,1)S(1)} copy-done((bf16[128,4096]{1,0:T(8,128)(2,1)S(1)}, bf16[128,4096]{1,0:T(8,128)(2,1)}, u32[]{:S(2)}) %copy-start.2) | copy-done | bytes 1048600
  2.6 0.0 copy-start.3
  2.6 1.2 %copy-done.3 = bf16[128,4096]{1,0:T(8,128)(2,1)S(1)} copy-done((bf16[128,4096]{1,0:T(8,128)(2,1)S(1)}, bf16[128,4096]{1,0:T(8,128)(2,1)}, u32[]{:S(2)}) %copy-start.3) | copy-done | bytes 1048600
  3.9 0.0 copy-start.4
  3.9 0.9 copy-done.4
  4.8 0.0 copy-start.5
  4.8 0.9 copy-done.5
  5.7 0.0 copy-start.6
  5.7 0.7 copy-done.6
  6.4 44.2 %move_and_gather.1 = (bf16[2,8,16,2048]{3,2,1,0:T(8,128)(2,1)S(1)}, bf16[2,128,2048]{2,1,0:T(8,128)(2,1)S(1)}, bf16[8,2,8,16,512]{4,3,2,1,0:T(8,128)(2,1)S(1)}, s32[256]{0:T(256)S(1)}) custom-call(bf16[8,16,4096]{2,1,0:T(8,128)(2,1)S(1)} %bitcast.13, bf16[8,16,512]{2,1,0:T(8,128)(2,1)S(1)} %bitcast.16, bf16[8,16,512]{2,1,0:T(8,128)(2,1)S(1)} %bitcast.17, ...), custom_call_target="tpu_custom_call" | custom-call | tf_op jit(solution)/shard_map/move_and_gather/pallas_call | solution.py:406
  50.6 0.0 copy-start
  50.6 1.3 %copy-done = bf16[8,2,8,16,512]{4,3,2,1,0:T(8,128)(2,1)} copy-done((bf16[8,2,8,16,512]{4,3,2,1,0:T(8,128)(2,1)}, bf16[8,2,8,16,512]{4,3,2,1,0:T(8,128)(2,1)S(1)}, u32[]{:S(2)}) %copy-start) | copy-done | bytes 2097176
  52.0 0.0 copy-done.7
  52.0 0.0 copy-done.8
  52.0 27.7 %attend.1 = (bf16[256,2048]{1,0:T(8,128)(2,1)S(1)}, bf16[256,2048]{1,0:T(8,128)(2,1)S(1)}, bf16[128,16,512]{2,1,0:T(8,128)(2,1)}) custom-call(s32[256]{0:T(256)S(1)} %get-tuple-element.11.table_ref, s32[8,8]{1,0:T(8,128)S(1)} %copy-done.8, s32[8,128]{1,0:T(8,128)S(1)} %copy-done.7, bf16[256,2048]{1,0:T(8,128)(2,1)S(1)} %bitcast.11, ...), custom_call_target="tpu_custom_call" | custom-call | tf_op jit(solution)/shard_map/attend/pallas_call | solution.py:432
  79.6 0.0 copy-start.1
  79.6 1.6 %copy-done.1 = bf16[128,16,512]{2,1,0:T(8,128)(2,1)S(1)} copy-done((bf16[128,16,512]{2,1,0:T(8,128)(2,1)S(1)}, bf16[128,16,512]{2,1,0:T(8,128)(2,1)}, u32[]{:S(2)}) %copy-start.1) | copy-done | bytes 2097176
  81.2 28.7 %reduce_and_share.1 = (bf16[128,4096]{1,0:T(8,128)(2,1)S(1)}, bf16[128,4096]{1,0:T(8,128)(2,1)S(1)}, bf16[128,512]{1,0:T(8,128)(2,1)S(1)}, bf16[128,512]{1,0:T(8,128)(2,1)S(1)}) custom-call(bf16[2,128,2048]{2,1,0:T(8,128)(2,1)S(1)} %bitcast.14, bf16[2,128,2048]{2,1,0:T(8,128)(2,1)S(1)} %bitcast.15, bf16[8,2,128,512]{3,2,1,0:T(8,128)(2,1)S(1)} %bitcast.10), custom_call_target="tpu_custom_call" | custom-call | tf_op jit(solution)/shard_map/reduce_and_share/pallas_call | solution.py:455
  109.9 1.0 copy.16
  110.9 1.0 copy.17
  111.9 0.7 copy.18
  112.5 0.7 copy.19
Async XLA Ops:
  0.6 51.3 %copy-start.7 = (s32[8,128]{1,0:T(8,128)S(1)}, s32[8,128]{1,0:T(8,128)}, u32[]{:S(2)}) copy-start(s32[8,128]{1,0:T(8,128)} %order_ref.3) | copy-start | bytes 12292
  0.6 51.3 %copy-start.8 = (s32[8,8]{1,0:T(8,128)S(1)}, s32[8,8]{1,0:T(8,128)}, u32[]{:S(2)}) copy-start(s32[8,8]{1,0:T(8,128)} %lengths_ref.1) | copy-start | bytes 772
  1.4 1.2 %copy-start.2 = (bf16[128,4096]{1,0:T(8,128)(2,1)S(1)}, bf16[128,4096]{1,0:T(8,128)(2,1)}, u32[]{:S(2)}) copy-start(bf16[128,4096]{1,0:T(8,128)(2,1)} %param.7) | copy-start | bytes 3145732
  2.6 1.2 %copy-start.3 = (bf16[128,4096]{1,0:T(8,128)(2,1)S(1)}, bf16[128,4096]{1,0:T(8,128)(2,1)}, u32[]{:S(2)}) copy-start(bf16[128,4096]{1,0:T(8,128)(2,1)} %do_ref.1) | copy-start | bytes 3145732
  3.9 0.9 copy-start.4
  4.8 0.9 copy-start.5
  5.7 0.7 copy-start.6
  50.6 1.3 %copy-start = (bf16[8,2,8,16,512]{4,3,2,1,0:T(8,128)(2,1)}, bf16[8,2,8,16,512]{4,3,2,1,0:T(8,128)(2,1)S(1)}, u32[]{:S(2)}) copy-start(bf16[8,2,8,16,512]{4,3,2,1,0:T(8,128)(2,1)S(1)} %get-tuple-element.14) | copy-start | bytes 6291460
  79.6 1.6 %copy-start.1 = (bf16[128,16,512]{2,1,0:T(8,128)(2,1)S(1)}, bf16[128,16,512]{2,1,0:T(8,128)(2,1)}, u32[]{:S(2)}) copy-start(bf16[128,16,512]{2,1,0:T(8,128)(2,1)} %get-tuple-element.17) | copy-start | bytes 6291460

commit v2 on v1

v2 whole, which is shorter than its diff:
```python
import functools
import math

import jax
import jax.numpy as jnp
from jax import lax
from jax.experimental import pallas as pl
from jax.experimental.pallas import tpu as pltpu
from jax.sharding import PartitionSpec as P

HEADS = 32
KEY_HEADS = 4
HEAD = 128
PER_KEY = 8
BLOCK = 16
ROWS = 128
GROUPS = 8
MEMBERS = 16
CHIPS = 8
GROUP_ROWS = 2048
HALF = HEADS * HEAD // 2
KEYS_HALF = KEY_HEADS * HEAD // 2
CHUNK = 128
MOST_CHUNKS = 9
DOCS = 8
TOGETHER = 2
SLOTS = GROUPS * MEMBERS
PIECES = 4
SCALE = 1.0 / math.sqrt(HEAD)
LOG2E = 1.4426950408889634
FILL = -1e30
MESH = pl.DeviceIdType.MESH
WHOLE = 56 << 20


def place():
    group = lax.axis_index("dp")
    member = lax.axis_index("fsdp")
    return group, member // 8, (member // 2) % 4, member % 2


def member_of(zh, x, core):
    return zh * 8 + x * 2 + core


def gather_kernel(
    q_ref, k_ref, v_ref, do_ref, shift_hbm, order_hbm, lengths_hbm,
    rq_ref, do2_ref, kv_ref, table_ref,
    shift_ref, order_ref, lengths_ref, counts, k_in, v_in, q_in, send_q, send_kv, own, q_land,
    in_sem, kv_ssem, kv_rsem, q_ssem, q_rsem, do_ssem, do_rsem, o_ssem, o_rsem, z_ssem, z_rsem, f_ssem, f_rsem, local_sem,
):
    group, zh, x, core = place()
    member = member_of(zh, x, core)
    chip = zh * 4 + x
    chip_z = (1 - zh) * 4 + x
    right, left = (x + 1) % 4, (x + 3) % 4
    other = 1 - core

    def peer(plane, col, side):
        return (group, member_of(plane, col, side))

    def remote(src, dst, ssem, rsem, dev):
        return pltpu.make_async_remote_copy(
            src_ref=src, dst_ref=dst, send_sem=ssem, recv_sem=rsem, device_id=dev, device_id_type=MESH
        )

    loads = [
        pltpu.make_async_copy(src, dst, in_sem.at[i])
        for i, (src, dst) in enumerate((
            (shift_hbm, shift_ref), (k_ref, k_in), (v_ref, v_in), (q_ref, q_in),
            (order_hbm, order_ref), (lengths_hbm, lengths_ref),
        ))
    ]
    for copy in loads:
        copy.start()

    barrier = pltpu.get_barrier_semaphore()
    greeted = 0
    for step in range(1, GROUPS):
        dev = ((group + GROUPS - step) % GROUPS, member)
        pl.semaphore_signal(barrier, inc=1, device_id=dev, device_id_type=MESH)
        greeted += 1
    around = [(1 - zh, x, 0), (1 - zh, x, 1)]
    for side in range(2):
        around += [(zh, right, side), (zh, left, side)]
    for spot in around + [(zh, x, other)]:
        pl.semaphore_signal(barrier, inc=1, device_id=peer(*spot), device_id_type=MESH)
        greeted += 1

    def block_for(row, step):
        found = jnp.int32(0)
        for b in range(GROUPS):
            found = jnp.maximum(found, jnp.where(shift_ref[b, row] == step, b, 0))
        return found

    loads[0].wait()
    blocks = [block_for(member, step) for step in range(GROUPS)]
    loads[1].wait()
    loads[2].wait()
    for step in range(GROUPS):
        for side in range(2):
            cols = slice(side * KEYS_HALF, (side + 1) * KEYS_HALF)
            send_kv[side, step, :, 0:KEYS_HALF] = k_in[blocks[step], :, cols]
            send_kv[side, step, :, KEYS_HALF:] = v_in[blocks[step], :, cols]

    pl.semaphore_wait(barrier, greeted)
    own_kv = pltpu.make_async_copy(send_kv.at[:, 0], own.at[:, 0], local_sem.at[0])
    own_kv.start()
    kv_copies = [
        remote(send_kv.at[:, s], own.at[:, s], kv_ssem.at[s], kv_rsem.at[s], ((group + s) % GROUPS, member))
        for s in range(1, GROUPS)
    ]
    for copy in kv_copies:
        copy.start()
    loads[3].wait()
    for step in range(GROUPS):
        send_q[step] = q_in[blocks[step]]

    def halves(ref, side):
        return ref.at[:, pl.ds(pl.multiple_of(side * HALF, HALF), HALF)]

    own_kv.wait()
    for copy in kv_copies:
        copy.wait_recv()
    def own_send(index, flip, dev_of):
        side = core if flip == 0 else other
        return remote(own.at[side], kv_ref.at[chip, core], o_ssem.at[index, flip], o_rsem.at[index, flip], dev_of(side))

    sends = []

    def go(copy):
        copy.start()
        sends.append(copy)
        return copy

    own_z = [go(own_send(0, f, lambda side: peer(1 - zh, x, side))) for f in range(2)]
    own_r = [go(own_send(1, f, lambda side: peer(zh, right, side))) for f in range(2)]
    own_l = [go(own_send(2, f, lambda side: peer(zh, left, side))) for f in range(2)]
    own_c = go(remote(own.at[other], kv_ref.at[chip, core], o_ssem.at[3, 0], o_rsem.at[3, 0], peer(zh, x, other)))
    own_here = pltpu.make_async_copy(own.at[core], kv_ref.at[chip, core], local_sem.at[1])
    own_here.start()

    def fill(row, carry):
        for step in range(GROUPS):
            b = block_for(row, step)
            table_ref[row * GROUPS + step] = order_ref[group, row * GROUPS + b]
        return carry

    loads[4].wait()
    loads[5].wait()
    lax.fori_loop(0, MEMBERS, fill, 0)
    for side in range(2):
        row = member_of(zh, x, side)
        for step in range(GROUPS):
            b = block_for(row, step)
            table_ref[128 + side * GROUPS + step] = order_ref[group, row * GROUPS + b]
            table_ref[144 + side * GROUPS + step] = b

    def count_chunks(index, carry):
        p = table_ref[128 + index] * BLOCK
        first = jnp.int32(0)
        end = jnp.int32(0)
        for e in range(DOCS):
            length = lengths_ref[group, e]
            end = end + length
            first = first + jnp.where(end <= p, length, 0)
        counts[index] = (p + BLOCK - 1) // CHUNK - first // CHUNK + 1
        return carry

    lax.fori_loop(0, 2 * GROUPS, count_chunks, 0)

    def rank_of(index, carry):
        mine = counts[index] * 16 + index
        rank = jnp.int32(0)
        for i in range(2 * GROUPS):
            rank = rank + jnp.where(counts[i] * 16 + i < mine, 1, 0)
        counts[16 + index] = rank
        return carry

    lax.fori_loop(0, 2 * GROUPS, rank_of, 0)

    def place_rank(rank, carry):
        found = jnp.int32(0)
        for i in range(2 * GROUPS):
            found = jnp.maximum(found, jnp.where(counts[16 + i] == rank, i, 0))
        table_ref[160 + rank] = found
        return carry

    lax.fori_loop(0, 2 * GROUPS, place_rank, 0)

    z_r, z_l = [None, None], [None, None]
    for f in range(2):
        own_z[f].wait_recv()
        src = kv_ref.at[chip_z, core if f == 0 else other]
        z_r[f] = go(remote(src, src, z_ssem.at[0, f], z_rsem.at[0, f], peer(zh, right, core)))
        z_l[f] = go(remote(src, src, z_ssem.at[1, f], z_rsem.at[1, f], peer(zh, left, core)))

    q_copies = [
        remote(send_q.at[s], q_land.at[s], q_ssem.at[s], q_rsem.at[s], ((group + s) % GROUPS, member))
        for s in range(1, GROUPS)
    ]
    for copy in q_copies[:3]:
        copy.start()
    do_copy = go(remote(halves(do_ref, other), do2_ref.at[core], do_ssem, do_rsem, peer(zh, x, other)))
    own_do = pltpu.make_async_copy(halves(do_ref, core), do2_ref.at[core], local_sem.at[2])
    own_do.start()

    own_r[0].wait_recv()
    src = kv_ref.at[zh * 4 + left, core]
    far_r = go(remote(src, src, f_ssem.at[0, 0], f_rsem.at[0, 0], peer(zh, right, core)))
    own_l[1].wait_recv()
    src = kv_ref.at[zh * 4 + right, other]
    far_l = go(remote(src, src, f_ssem.at[0, 1], f_rsem.at[0, 1], peer(zh, left, core)))
    for copy in q_copies[3:]:
        copy.start()
    own_r[1].wait_recv()
    own_l[0].wait_recv()
    z_r[0].wait_recv()
    src = kv_ref.at[(1 - zh) * 4 + left, core]
    zfar_r = go(remote(src, src, f_ssem.at[1, 0], f_rsem.at[1, 0], peer(zh, right, core)))
    z_l[1].wait_recv()
    src = kv_ref.at[(1 - zh) * 4 + right, other]
    zfar_l = go(remote(src, src, f_ssem.at[1, 1], f_rsem.at[1, 1], peer(zh, left, core)))

    def half_cols(ref, side):
        return ref.at[:, :, pl.ds(pl.multiple_of(side * HALF, HALF), HALF)]

    send_self = pltpu.make_async_copy(send_q.at[0], q_land.at[0], local_sem.at[3])
    send_self.start()
    send_self.wait()
    for copy in q_copies:
        copy.wait_recv()
        sends.append(copy)
    q_swap = go(remote(half_cols(q_land, other), rq_ref.at[core], q_ssem.at[0], q_rsem.at[0], peer(zh, x, other)))
    q_here = pltpu.make_async_copy(half_cols(q_land, core), rq_ref.at[core], local_sem.at[4])
    q_here.start()
    z_r[1].wait_recv()
    z_l[0].wait_recv()
    own_c.wait_recv()
    do_copy.wait_recv()
    for copy in (far_r, far_l, zfar_r, zfar_l):
        copy.wait_recv()
    q_swap.wait_recv()
    q_here.wait()
    own_do.wait()
    own_here.wait()
    for copy in kv_copies + sends:
        copy.wait_send()


def attend_kernel(
    table_ref, lengths_ref, order_ref, rq_hbm, do_hbm, kv_hbm,
    attn_hbm, dq_hbm, dkv_hbm,
    rq_ref, do_ref, kv_ref, attn_ref, dq_ref, dkv_ref, ks, acc, turned, in_sem, out_sem,
):
    group = lax.axis_index("dp")
    pieces = [pl.ds(i * SLOTS // PIECES, SLOTS // PIECES) for i in range(PIECES)]
    kv_loads = [
        pltpu.make_async_copy(kv_hbm.at[piece], kv_ref.at[piece], in_sem.at[2 + i]) for i, piece in enumerate(pieces)
    ]
    loads = [pltpu.make_async_copy(rq_hbm, rq_ref, in_sem.at[0]), pltpu.make_async_copy(do_hbm, do_ref, in_sem.at[1])]
    for copy in kv_loads + loads:
        copy.start()

    def arrange(slot, carry):
        dst = pl.multiple_of(table_ref[slot] * BLOCK, BLOCK)
        ks[pl.ds(dst, BLOCK), :] = kv_ref[slot]
        return carry

    acc[...] = jnp.zeros_like(acc)
    for i, copy in enumerate(kv_loads):
        copy.wait()
        lax.fori_loop(i * SLOTS // PIECES, (i + 1) * SLOTS // PIECES, arrange, 0, unroll=8)
    for copy in loads:
        copy.wait()

    def describe(index):
        p = table_ref[128 + index]
        out_row = pl.multiple_of((index // GROUPS) * ROWS + table_ref[144 + index] * BLOCK, BLOCK)
        in_row = pl.multiple_of(index * BLOCK, BLOCK)
        first = jnp.int32(0)
        end = jnp.int32(0)
        for e in range(DOCS):
            length = lengths_ref[group, e]
            end = end + length
            first = first + jnp.where(end <= p * BLOCK, length, 0)
        low = first // CHUNK
        count = (p * BLOCK + BLOCK - 1) // CHUNK - low + 1
        return p, in_row, out_row, low, count

    def tile(x, width):
        return (x.reshape(PER_KEY, BLOCK, width))

    def run(n, items):
        width = n * CHUNK
        lanes = lax.broadcasted_iota(jnp.int32, (BLOCK, CHUNK), 1)
        chains = []
        for p, in_row, out_row, low, count in items:
            pos = p * BLOCK + lax.broadcasted_iota(jnp.int32, (BLOCK, CHUNK), 0)
            start = jnp.zeros((BLOCK, CHUNK), jnp.int32)
            end = jnp.int32(0)
            for e in range(DOCS):
                length = lengths_ref[group, e]
                end = end + length
                start = start + jnp.where(end <= pos, length, 0)
            base = pl.multiple_of(jnp.minimum(low, GROUP_ROWS // CHUNK - n) * CHUNK, CHUNK)
            keys = pl.ds(base, width)
            parts = []
            for c in range(n):
                key = base + c * CHUNK + lanes
                parts.append(jnp.where((key >= start) & (key <= pos), 0.0, FILL).astype(jnp.float32))
            bias = jnp.concatenate(parts, axis=1) if n > 1 else parts[0]
            for h in range(2):
                def heads(ref, row):
                    return jnp.concatenate(
                        [ref[pl.ds(row, BLOCK), pl.ds((h * PER_KEY + g) * HEAD, HEAD)] for g in range(PER_KEY)], axis=0
                    )
                d = dict(h=h, keys=keys, bias=bias, out_row=out_row)
                d['q'] = heads(rq_ref, in_row)
                d['do'] = heads(do_ref, out_row)
                d['k'] = lambda d=d: ks[d['keys'], pl.ds(d['h'] * HEAD, HEAD)]
                d['v'] = lambda d=d: ks[d['keys'], pl.ds(KEYS_HALF + d['h'] * HEAD, HEAD)]
                chains.append(d)
        for d in chains:
            s = lax.dot_general(d['q'], d['k'](), (((1,), (1,)), ((), ())), preferred_element_type=jnp.float32)
            d['s'] = (tile(s, width) + d['bias'][None]).reshape(PER_KEY * BLOCK, width)
        for d in chains:
            d['top'] = jnp.max(d['s'], axis=1, keepdims=True)
        for d in chains:
            d['dp'] = lax.dot_general(d['do'], d['v'](), (((1,), (1,)), ((), ())), preferred_element_type=jnp.float32)
        for d in chains:
            w = jnp.exp2((d['s'] - d['top']) * (SCALE * LOG2E))
            d['w'] = w
            d['inv'] = 1.0 / jnp.sum(w, axis=1, keepdims=True)
            d['wl'] = w.astype(jnp.bfloat16)
        for d in chains:
            out = lax.dot_general(d['wl'], d['v'](), (((1,), (0,)), ((), ())), preferred_element_type=jnp.float32)
            d['out'] = (out * d['inv']).astype(jnp.bfloat16)
            dw = d['do'].astype(jnp.float32)
            d['delta'] = jnp.sum(dw * d['out'].astype(jnp.float32), axis=1, keepdims=True)
            d['qs'] = (d['q'].astype(jnp.float32) * (d['inv'] * SCALE)).astype(jnp.bfloat16)
            d['dos'] = (dw * d['inv']).astype(jnp.bfloat16)
        for d in chains:
            acc[d['h'], 1, :, d['keys']] += lax.dot_general(
                d['dos'], d['wl'], (((0,), (0,)), ((), ())), preferred_element_type=jnp.float32
            )
        for d in chains:
            d['ds'] = (d['w'] * (d['dp'] - d['delta'])).astype(jnp.bfloat16)
        for d in chains:
            gq = lax.dot_general(d['ds'], d['k'](), (((1,), (0,)), ((), ())), preferred_element_type=jnp.float32)
            d['gq'] = (gq * (d['inv'] * SCALE)).astype(jnp.bfloat16)
        for d in chains:
            acc[d['h'], 0, :, d['keys']] += lax.dot_general(
                d['qs'], d['ds'], (((0,), (0,)), ((), ())), preferred_element_type=jnp.float32
            )
        for d in chains:
            for g in range(PER_KEY):
                cols = pl.ds((d['h'] * PER_KEY + g) * HEAD, HEAD)
                attn_ref[pl.ds(d['out_row'], BLOCK), cols] = d['out'][g * BLOCK:(g + 1) * BLOCK]
                dq_ref[pl.ds(d['out_row'], BLOCK), cols] = d['gq'][g * BLOCK:(g + 1) * BLOCK]

    def item(step, carry):
        items = [describe(table_ref[160 + step * TOGETHER + i]) for i in range(TOGETHER)]
        count = items[0][4]
        for it in items[1:]:
            count = jnp.maximum(count, it[4])
        for n in range(1, MOST_CHUNKS + 1):
            pl.when(count == n)(functools.partial(run, n, items))
        return carry

    lax.fori_loop(0, 2 * GROUPS // TOGETHER, item, 0)
    stores = [
        pltpu.make_async_copy(attn_ref, attn_hbm, out_sem.at[0]), pltpu.make_async_copy(dq_ref, dq_hbm, out_sem.at[1])
    ]
    for copy in stores:
        copy.start()

    def turn(c, carry):
        keys = pl.ds(pl.multiple_of(c * CHUNK, CHUNK), CHUNK)
        for h in range(2):
            for which in range(2):
                turned[keys, pl.ds(which * KEYS_HALF + h * HEAD, HEAD)] = acc[h, which, :, keys].T.astype(jnp.bfloat16)
        return carry

    lax.fori_loop(0, GROUP_ROWS // CHUNK, turn, 0)

    def restore(slot, carry):
        src = pl.multiple_of(order_ref[group, slot] * BLOCK, BLOCK)
        dkv_ref[slot] = turned[pl.ds(src, BLOCK), :]
        return carry

    for i, piece in enumerate(pieces):
        lax.fori_loop(i * SLOTS // PIECES, (i + 1) * SLOTS // PIECES, restore, 0, unroll=8)
        copy = pltpu.make_async_copy(dkv_ref.at[piece], dkv_hbm.at[piece], out_sem.at[2 + i])
        copy.start()
        stores.append(copy)
    for copy in stores:
        copy.wait()


def scatter_kernel(
    attn2_ref, dq2_ref, u_hbm,
    attn_ref, dq_ref, grads_ref,
    u_ref, z0_in, far_out, far_in, cross_in, near_out, near_in, z1_out, z1_in, total,
    o_ssem, o_rsem, z_ssem, z_rsem, f_ssem, f_rsem, c_ssem, c_rsem, n_ssem, n_rsem, local_sem, u_sem,
):
    u_load = pltpu.make_async_copy(u_hbm, u_ref, u_sem)
    u_load.start()
    group, zh, x, core = place()
    right, left, across = (x + 1) % 4, (x + 3) % 4, (x + 2) % 4
    other = 1 - core
    z_peer = (group, member_of(1 - zh, x, core))
    r_peer = (group, member_of(zh, right, core))
    l_peer = (group, member_of(zh, left, core))
    core_peer = (group, member_of(zh, x, other))
    barrier = pltpu.get_barrier_semaphore()
    for dev in (z_peer, r_peer, l_peer, core_peer):
        pl.semaphore_signal(barrier, inc=1, device_id=dev, device_id_type=MESH)
    pl.semaphore_wait(barrier, 4)
    sends = []

    def go(src, dst, ssem, rsem, dev):
        copy = pltpu.make_async_remote_copy(
            src_ref=src, dst_ref=dst, send_sem=ssem, recv_sem=rsem, device_id=dev, device_id_type=MESH
        )
        copy.start()
        sends.append(copy)
        return copy

    def wide(value):
        return value.astype(jnp.float32)

    here, there = zh * 4, (1 - zh) * 4
    sides = ((0, r_peer, right), (1, l_peer, left))
    z0 = go(u_hbm.at[there + across], z0_in, z_ssem.at[0], z_rsem.at[0], z_peer)
    cross = [go(u_hbm.at[there + to], cross_in.at[d], c_ssem.at[d], c_rsem.at[d], dev) for d, dev, to in sides]
    outs = [
        go(src.at[other], dst, o_ssem.at[i], o_rsem.at[i], core_peer)
        for i, (src, dst) in enumerate(((attn2_ref, attn_ref), (dq2_ref, dq_ref)))
    ]
    u_load.wait()
    z0.wait_recv()
    far = []
    for d, dev, to in sides:
        far_out[d] = (wide(u_ref[here + across, d]) + wide(z0_in[d])).astype(jnp.bfloat16)
        far.append(go(far_out.at[d], far_in.at[d], f_ssem.at[d], f_rsem.at[d], dev))
    near = []
    for d, dev, to in sides:
        near.append(go(u_ref.at[here + to, 1 - d], near_in.at[d, 1 - d], n_ssem.at[d, 0], n_rsem.at[d, 0], dev))
    for copy in cross:
        copy.wait_recv()
    z1_out[...] = (wide(u_ref[there + x]) + wide(cross_in[0]) + wide(cross_in[1])).astype(jnp.bfloat16)
    z1 = go(z1_out, z1_in, z_ssem.at[1], z_rsem.at[1], z_peer)
    for d, dev, to in sides:
        far[d].wait_recv()
        near_out[d] = (wide(u_ref[here + to, d]) + wide(far_in[d])).astype(jnp.bfloat16)
        near.append(go(near_out.at[d], near_in.at[d, d], n_ssem.at[d, 1], n_rsem.at[d, 1], dev))
    z1.wait_recv()
    for copy in near:
        copy.wait_recv()
    total[...] = (
        wide(u_ref[here + x]) + wide(z1_in[...]) + wide(near_in[0]) + wide(near_in[1])
    ).astype(jnp.bfloat16)
    last = go(total.at[other], grads_ref.at[core], o_ssem.at[2], o_rsem.at[2], core_peer)
    kept = pltpu.make_async_copy(total.at[core], grads_ref.at[core], local_sem)
    kept.start()
    for copy in outs:
        copy.wait_recv()
    last.wait_recv()
    kept.wait()
    for copy in sends:
        copy.wait_send()


def finish_kernel(
    attn2_ref, dq2_ref, attn_in, dq_in, grads_in, attn_ref, dq_ref, gk_ref, gv_ref, wide, narrow, in_sem, out_sem,
):
    core = lax.axis_index("fsdp") % 2

    def cols(ref, side, width):
        return ref.at[:, pl.ds(pl.multiple_of(side * width, width), width)]

    groups = [
        (grads_in, narrow, [
            (narrow.at[side, :, pl.ds(which * KEYS_HALF, KEYS_HALF)], cols(dst, side, KEYS_HALF))
            for side in range(2) for which, dst in enumerate((gk_ref, gv_ref))
        ]),
        (attn2_ref.at[core], wide.at[0], [(wide.at[0], cols(attn_ref, core, HALF))]),
        (dq2_ref.at[core], wide.at[1], [(wide.at[1], cols(dq_ref, core, HALF))]),
        (attn_in, wide.at[2], [(wide.at[2], cols(attn_ref, 1 - core, HALF))]),
        (dq_in, wide.at[3], [(wide.at[3], cols(dq_ref, 1 - core, HALF))]),
    ]
    loads = [pltpu.make_async_copy(src, here, in_sem.at[i]) for i, (src, here, _) in enumerate(groups)]
    for copy in loads:
        copy.start()
    stores = []
    for copy, (_, _, pairs) in zip(loads, groups):
        copy.wait()
        for src, dst in pairs:
            out = pltpu.make_async_copy(src, dst, out_sem.at[len(stores)])
            out.start()
            stores.append(out)
    for copy in stores:
        copy.wait()


VMEM = pl.BlockSpec(memory_space=pltpu.VMEM)
SMEM = pl.BlockSpec(memory_space=pltpu.SMEM)
ANY = pl.BlockSpec(memory_space=pl.ANY)
HBM = pl.BlockSpec(memory_space=pltpu.HBM)


def on_device(queries, keys, values, output_gradient, doc_lengths, block_order, group_shift):
    low = jnp.bfloat16
    dma = pltpu.SemaphoreType.DMA
    rq, do2, kv, table = pl.pallas_call(
        gather_kernel,
        out_shape=(
            jax.ShapeDtypeStruct((2, GROUPS, BLOCK, HALF), low),
            jax.ShapeDtypeStruct((2, ROWS, HALF), low),
            jax.ShapeDtypeStruct((CHIPS, 2, GROUPS, BLOCK, 2 * KEYS_HALF), low),
            jax.ShapeDtypeStruct((256,), jnp.int32),
        ),
        in_specs=[HBM] * 7,
        out_specs=(ANY, ANY, ANY, SMEM),
        scratch_shapes=[
            pltpu.SMEM((GROUPS, MEMBERS), jnp.int32),
            pltpu.SMEM((GROUPS, MEMBERS * GROUPS), jnp.int32),
            pltpu.SMEM((GROUPS, DOCS), jnp.int32),
            pltpu.SMEM((32,), jnp.int32),
            pltpu.VMEM((GROUPS, BLOCK, 2 * KEYS_HALF), low),
            pltpu.VMEM((GROUPS, BLOCK, 2 * KEYS_HALF), low),
            pltpu.VMEM((GROUPS, BLOCK, 2 * HALF), low),
            pltpu.VMEM((GROUPS, BLOCK, 2 * HALF), low),
            pltpu.VMEM((2, GROUPS, BLOCK, 2 * KEYS_HALF), low),
            pltpu.VMEM((2, GROUPS, BLOCK, 2 * KEYS_HALF), low),
            pltpu.VMEM((GROUPS, BLOCK, 2 * HALF), low),
            dma((6,)),
            dma((GROUPS,)), dma((GROUPS,)),
            dma((GROUPS,)), dma((GROUPS,)),
            dma, dma,
            dma((4, 2)), dma((4, 2)),
            dma((2, 2)), dma((2, 2)),
            dma((2, 2)), dma((2, 2)),
            dma((5,)),
        ],
        compiler_params=pltpu.CompilerParams(collective_id=1, has_side_effects=True, vmem_limit_bytes=WHOLE),
        name="move_and_gather",
    )(
        queries.reshape(GROUPS, BLOCK, 2 * HALF), keys.reshape(GROUPS, BLOCK, 2 * KEYS_HALF),
        values.reshape(GROUPS, BLOCK, 2 * KEYS_HALF), output_gradient, group_shift.T, block_order, doc_lengths,
    )

    attn2, dq2, dkv = pl.pallas_call(
        attend_kernel,
        out_shape=(
            jax.ShapeDtypeStruct((2 * ROWS, HALF), low),
            jax.ShapeDtypeStruct((2 * ROWS, HALF), low),
            jax.ShapeDtypeStruct((SLOTS, BLOCK, 2 * KEYS_HALF), low),
        ),
        in_specs=[SMEM, SMEM, SMEM, ANY, ANY, ANY],
        out_specs=(ANY, ANY, ANY),
        scratch_shapes=[
            pltpu.VMEM((2 * ROWS, HALF), low), pltpu.VMEM((2 * ROWS, HALF), low),
            pltpu.VMEM((SLOTS, BLOCK, 2 * KEYS_HALF), low),
            pltpu.VMEM((2 * ROWS, HALF), low), pltpu.VMEM((2 * ROWS, HALF), low),
            pltpu.VMEM((SLOTS, BLOCK, 2 * KEYS_HALF), low),
            pltpu.VMEM((GROUP_ROWS, 2 * KEYS_HALF), low),
            pltpu.VMEM((2, 2, HEAD, GROUP_ROWS), jnp.float32),
            pltpu.VMEM((GROUP_ROWS, 2 * KEYS_HALF), low),
            dma((2 + PIECES,)), dma((2 + PIECES,)),
        ],
        compiler_params=pltpu.CompilerParams(vmem_limit_bytes=WHOLE),
        name="attend",
    )(
        table, doc_lengths, block_order,
        rq.reshape(2 * ROWS, HALF), do2.reshape(2 * ROWS, HALF),
        kv.reshape(SLOTS, BLOCK, 2 * KEYS_HALF),
    )
    attn2 = attn2.reshape(2, ROWS, HALF)
    dq2 = dq2.reshape(2, ROWS, HALF)

    region = (2, ROWS, 2 * KEYS_HALF)
    attn_in, dq_in, grads = pl.pallas_call(
        scatter_kernel,
        out_shape=(
            jax.ShapeDtypeStruct((ROWS, HALF), low),
            jax.ShapeDtypeStruct((ROWS, HALF), low),
            jax.ShapeDtypeStruct(region, low),
        ),
        in_specs=[ANY, ANY, ANY],
        out_specs=(ANY, ANY, ANY),
        scratch_shapes=[
            pltpu.VMEM((CHIPS,) + region, low),
            pltpu.VMEM(region, low),
            pltpu.VMEM(region, low), pltpu.VMEM(region, low),
            pltpu.VMEM((2,) + region, low),
            pltpu.VMEM(region, low), pltpu.VMEM((2,) + region, low),
            pltpu.VMEM(region, low), pltpu.VMEM(region, low),
            pltpu.VMEM(region, low),
            dma((3,)), dma((3,)),
            dma((2,)), dma((2,)),
            dma((2,)), dma((2,)),
            dma((2,)), dma((2,)),
            dma((2, 2)), dma((2, 2)),
            dma, dma,
        ],
        compiler_params=pltpu.CompilerParams(collective_id=2, has_side_effects=True, vmem_limit_bytes=WHOLE),
        name="reduce_and_share",
    )(attn2, dq2, dkv.reshape((CHIPS,) + region))

    return pl.pallas_call(
        finish_kernel,
        out_shape=(
            jax.ShapeDtypeStruct((ROWS, 2 * HALF), low),
            jax.ShapeDtypeStruct((ROWS, 2 * HALF), low),
            jax.ShapeDtypeStruct((ROWS, 2 * KEYS_HALF), low),
            jax.ShapeDtypeStruct((ROWS, 2 * KEYS_HALF), low),
        ),
        in_specs=[ANY] * 5,
        out_specs=(ANY,) * 4,
        scratch_shapes=[pltpu.VMEM((4, ROWS, HALF), low), pltpu.VMEM(region, low), dma((5,)), dma((8,))],
        compiler_params=pltpu.CompilerParams(vmem_limit_bytes=WHOLE),
        name="finish",
    )(attn2, dq2, attn_in, dq_in, grads)


def solution(mesh):
    rows = P(("dp", "fsdp"), None)
    return jax.shard_map(
        on_device,
        mesh=mesh,
        in_specs=(rows, rows, rows, rows, P(), P(), P()),
        out_specs=(rows, rows, rows, rows),
        check_vma=False,
    )
```

time: 114 us -> 81.9 us (0.72)
  Pallas kernels: 101 us -> 80.8 us
  local copies, waits for them, and re-layouts: 11.9 us -> 0 us
    unnamed x23 -> x0, local copies, waits for them, and re-layouts: 11.9 us -> none
    pallas_call x1, Pallas kernels: 27.7 us -> 16.6 us  [on_device(): pl.pallas_call(attend_kernel, out_shape=(jax.ShapeDtypeStruct((2 * ROWS,...]
    pallas_call x1, Pallas kernels: 44.2 us -> 39.2 us  [on_device(): pl.pallas_call(gather_kernel, out_shape=(jax.ShapeDtypeStruct((2, GROUPS,...]
    pallas_call x1 -> x2, Pallas kernels: 28.7 us -> 24.9 us  [the longest x1 22.4 us: on_device(): pl.pallas_call(scatter_kernel, out_shape=(jax.ShapeDtypeStruct((ROWS, HAL...]
where the time goes in v2:
time: 81.9 us; the launch traced here: 81.4 us
  Pallas kernels  80.8 us (99%)
    pallas_call x1, Pallas kernels, on_device(): pl.pallas_call(gather_kernel, out_shape=(jax.ShapeDtypeStruct((2, GROUPS,...  39.2 us
    pallas_call x1, Pallas kernels, on_device(): pl.pallas_call(scatter_kernel, out_shape=(jax.ShapeDtypeStruct((ROWS, HAL...  22.4 us
    pallas_call x1, Pallas kernels, on_device(): pl.pallas_call(attend_kernel, out_shape=(jax.ShapeDtypeStruct((2 * ROWS,...  16.6 us
    pallas_call x1, Pallas kernels, on_device(): pl.pallas_call(finish_kernel, out_shape=(jax.ShapeDtypeStruct((ROWS, 2 *...  2.55 us

profile of v2, /device:TPU:1, one launch (start us, length us, event | category | flops | bytes accessed | tf_op | source)
XLA Modules:
  0.0 81.4 jit_solution(14953904669641464848)
XLA Ops:
  0.6 39.2 %move_and_gather.1 = (bf16[2,8,16,2048]{3,2,1,0:T(8,128)(2,1)}, bf16[2,128,2048]{2,1,0:T(8,128)(2,1)}, bf16[8,2,8,16,512]{4,3,2,1,0:T(8,128)(2,1)}, s32[256]{0:T(256)}) custom-call(bf16[8,16,4096]{2,1,0:T(8,128)(2,1)} %bitcast.18, bf16[8,16,512]{2,1,0:T(8,128)(2,1)} %bitcast.19, bf16[8,16,512]{2,1,0:T(8,128)(2,1)} %bitcast.20, bf16[128,4096]{1,0:T(8,128)(2,1)} %do_ref.1, ...), custom_call_target="tpu_custom_call" | custom-call | tf_op jit(solution)/shard_map/move_and_gather/pallas_call | solution.py:516
  39.8 16.6 %attend.1 = (bf16[256,2048]{1,0:T(8,128)(2,1)}, bf16[256,2048]{1,0:T(8,128)(2,1)}, bf16[128,16,512]{2,1,0:T(8,128)(2,1)}) custom-call(s32[256]{0:T(256)} %get-tuple-element.14.table_ref, s32[8,8]{1,0:T(8,128)} %lengths_ref.1, s32[8,128]{1,0:T(8,128)} %order_ref.1, bf16[256,2048]{1,0:T(8,128)(2,1)} %bitcast.16, bf16[256,2048]{1,0:T(8,128)(2,1)} %bitcast.17, ...), custom_call_target="tpu_custom_call" | custom-call | tf_op jit(solution)/shard_map/attend/pallas_call | solution.py:554
  56.5 22.4 %reduce_and_share.1 = (bf16[128,2048]{1,0:T(8,128)(2,1)}, bf16[128,2048]{1,0:T(8,128)(2,1)}, bf16[2,128,512]{2,1,0:T(8,128)(2,1)}) custom-call(bf16[2,128,2048]{2,1,0:T(8,128)(2,1)} %bitcast.10, bf16[2,128,2048]{2,1,0:T(8,128)(2,1)} %bitcast.12, bf16[8,2,128,512]{3,2,1,0:T(8,128)(2,1)} %bitcast.15), custom_call_target="tpu_custom_call" | custom-call | tf_op jit(solution)/shard_map/reduce_and_share/pallas_call | solution.py:584
  78.9 2.6 %finish.1 = (bf16[128,4096]{1,0:T(8,128)(2,1)}, bf16[128,4096]{1,0:T(8,128)(2,1)}, bf16[128,512]{1,0:T(8,128)(2,1)}, bf16[128,512]{1,0:T(8,128)(2,1)}) custom-call(bf16[2,128,2048]{2,1,0:T(8,128)(2,1)} %bitcast.11, bf16[2,128,2048]{2,1,0:T(8,128)(2,1)} %bitcast.13, bf16[128,2048]{1,0:T(8,128)(2,1)} %get-tuple-element.21.attn_in, ...), custom_call_target="tpu_custom_call" | custom-call | tf_op jit(solution)/shard_map/finish/pallas_call | solution.py:612

commit v3 on v2

--- a/solution.py
+++ b/solution.py
@@ -46,8 +46,8 @@
 def gather_kernel(
     q_ref, k_ref, v_ref, do_ref, shift_hbm, order_hbm, lengths_hbm,
     rq_ref, do2_ref, kv_ref, table_ref,
-    shift_ref, order_ref, lengths_ref, counts, k_in, v_in, q_in, send_q, send_kv, own, q_land,
-    in_sem, kv_ssem, kv_rsem, q_ssem, q_rsem, do_ssem, do_rsem, o_ssem, o_rsem, z_ssem, z_rsem, f_ssem, f_rsem, local_sem,
+    shift_ref, order_ref, lengths_ref, counts, k_in, v_in, q_in, send_q, send_kv, own,
+    in_sem, kv_ssem, kv_rsem, q_ssem, q_rsem, do_ssem, do_rsem, o_ssem, o_rsem, c_sem, z_ssem, z_rsem, f_ssem, f_rsem, local_sem,
 ):
     group, zh, x, core = place()
     member = member_of(zh, x, core)
@@ -74,12 +74,19 @@
     for copy in loads:
         copy.start()
 
+    def target(slot):
+        return ((group // 4 + slot // 4) % 2) * 4 + (group % 4 + slot % 4) % 4
+
+    def origin(slot):
+        return ((group // 4 + slot // 4) % 2) * 4 + (group % 4 + 4 - slot % 4) % 4
+
     barrier = pltpu.get_barrier_semaphore()
     greeted = 0
-    for step in range(1, GROUPS):
-        dev = ((group + GROUPS - step) % GROUPS, member)
-        pl.semaphore_signal(barrier, inc=1, device_id=dev, device_id_type=MESH)
-        greeted += 1
+    for slot in range(1, GROUPS):
+        for side in range(2):
+            dev = (origin(slot), member_of(zh, x, side))
+            pl.semaphore_signal(barrier, inc=1, device_id=dev, device_id_type=MESH)
+            greeted += 1
     around = [(1 - zh, x, 0), (1 - zh, x, 1)]
     for side in range(2):
         around += [(zh, right, side), (zh, left, side)]
@@ -94,7 +101,7 @@
         return found
 
     loads[0].wait()
-    blocks = [block_for(member, step) for step in range(GROUPS)]
+    blocks = [block_for(member, (target(slot) + GROUPS - group) % GROUPS) for slot in range(GROUPS)]
     loads[1].wait()
     loads[2].wait()
     for step in range(GROUPS):
@@ -107,7 +114,7 @@
     own_kv = pltpu.make_async_copy(send_kv.at[:, 0], own.at[:, 0], local_sem.at[0])
     own_kv.start()
     kv_copies = [
-        remote(send_kv.at[:, s], own.at[:, s], kv_ssem.at[s], kv_rsem.at[s], ((group + s) % GROUPS, member))
+        remote(send_kv.at[:, s], own.at[:, s], kv_ssem.at[s], kv_rsem.at[s], (target(s), member))
         for s in range(1, GROUPS)
     ]
     for copy in kv_copies:
@@ -119,12 +126,8 @@
     def halves(ref, side):
         return ref.at[:, pl.ds(pl.multiple_of(side * HALF, HALF), HALF)]
 
-    own_kv.wait()
-    for copy in kv_copies:
-        copy.wait_recv()
-    def own_send(index, flip, dev_of):
-        side = core if flip == 0 else other
-        return remote(own.at[side], kv_ref.at[chip, core], o_ssem.at[index, flip], o_rsem.at[index, flip], dev_of(side))
+    def half_cols(ref, side):
+        return ref.at[:, pl.ds(pl.multiple_of(side * HALF, HALF), HALF)]
 
     sends = []
 
@@ -133,17 +136,51 @@
         sends.append(copy)
         return copy
 
-    own_z = [go(own_send(0, f, lambda side: peer(1 - zh, x, side))) for f in range(2)]
-    own_r = [go(own_send(1, f, lambda side: peer(zh, right, side))) for f in range(2)]
-    own_l = [go(own_send(2, f, lambda side: peer(zh, left, side))) for f in range(2)]
-    own_c = go(remote(own.at[other], kv_ref.at[chip, core], o_ssem.at[3, 0], o_rsem.at[3, 0], peer(zh, x, other)))
+    def q_send(slot, flip):
+        side = core if flip == 0 else other
+        return go(remote(
+            half_cols(send_q.at[slot], side), rq_ref.at[core, slot],
+            q_ssem.at[slot, flip], q_rsem.at[slot, flip], (target(slot), member_of(zh, x, side)),
+        ))
+
+    def own_send(index, flip, part, spot):
+        side = core if flip == 0 else other
+        some = pl.ds(part * 4, 4)
+        return go(remote(
+            own.at[side, some], kv_ref.at[chip, core, some],
+            o_ssem.at[index, flip, part], o_rsem.at[index, flip, part], peer(*spot, side),
+        ))
+
+    own_kv.wait()
+    own_z, own_r, own_l = {}, {}, {}
+    arrived = 0
+    for part in range(2):
+        while arrived < (3, 7)[part]:
+            kv_copies[arrived].wait_recv()
+            arrived += 1
+        for f in range(2):
+            own_z[f, part] = own_send(0, f, part, (1 - zh, x))
+            own_r[f, part] = own_send(1, f, part, (zh, right))
+            own_l[f, part] = own_send(2, f, part, (zh, left))
+    q_copies = [q_send(slot, flip) for slot in range(1, 4) for flip in range(2)]
+    own_c = go(remote(own.at[other], kv_ref.at[chip, core], c_sem.at[0], c_sem.at[1], peer(zh, x, other)))
     own_here = pltpu.make_async_copy(own.at[core], kv_ref.at[chip, core], local_sem.at[1])
     own_here.start()
+    q_copies.append(q_send(0, 1))
+    q_here = pltpu.make_async_copy(half_cols(send_q.at[0], core), rq_ref.at[core, 0], local_sem.at[3])
+    q_here.start()
+    do_copy = go(remote(halves(do_ref, other), do2_ref.at[core], do_ssem, do_rsem, peer(zh, x, other)))
+    own_do = pltpu.make_async_copy(halves(do_ref, core), do2_ref.at[core], local_sem.at[2])
+    own_do.start()
+
+    def came(copies, f):
+        for part in range(2):
+            copies[f, part].wait_recv()
 
     def fill(row, carry):
-        for step in range(GROUPS):
-            b = block_for(row, step)
-            table_ref[row * GROUPS + step] = order_ref[group, row * GROUPS + b]
+        for slot in range(GROUPS):
+            b = block_for(row, (group + GROUPS - origin(slot)) % GROUPS)
+            table_ref[row * GROUPS + slot] = order_ref[group, row * GROUPS + b]
         return carry
 
     loads[4].wait()
@@ -151,10 +188,10 @@
     lax.fori_loop(0, MEMBERS, fill, 0)
     for side in range(2):
         row = member_of(zh, x, side)
-        for step in range(GROUPS):
-            b = block_for(row, step)
-            table_ref[128 + side * GROUPS + step] = order_ref[group, row * GROUPS + b]
-            table_ref[144 + side * GROUPS + step] = b
+        for slot in range(GROUPS):
+            b = block_for(row, (group + GROUPS - origin(slot)) % GROUPS)
+            table_ref[128 + side * GROUPS + slot] = order_ref[group, row * GROUPS + b]
+            table_ref[144 + side * GROUPS + slot] = b
 
     def count_chunks(index, carry):
         p = table_ref[128 + index] * BLOCK
@@ -190,31 +227,20 @@
 
     z_r, z_l = [None, None], [None, None]
     for f in range(2):
-        own_z[f].wait_recv()
+        came(own_z, f)
         src = kv_ref.at[chip_z, core if f == 0 else other]
         z_r[f] = go(remote(src, src, z_ssem.at[0, f], z_rsem.at[0, f], peer(zh, right, core)))
         z_l[f] = go(remote(src, src, z_ssem.at[1, f], z_rsem.at[1, f], peer(zh, left, core)))
 
-    q_copies = [
-        remote(send_q.at[s], q_land.at[s], q_ssem.at[s], q_rsem.at[s], ((group + s) % GROUPS, member))
-        for s in range(1, GROUPS)
-    ]
-    for copy in q_copies[:3]:
-        copy.start()
-    do_copy = go(remote(halves(do_ref, other), do2_ref.at[core], do_ssem, do_rsem, peer(zh, x, other)))
-    own_do = pltpu.make_async_copy(halves(do_ref, core), do2_ref.at[core], local_sem.at[2])
-    own_do.start()
-
-    own_r[0].wait_recv()
+    q_copies += [q_send(slot, flip) for slot in range(4, GROUPS) for flip in range(2)]
+    came(own_r, 0)
     src = kv_ref.at[zh * 4 + left, core]
     far_r = go(remote(src, src, f_ssem.at[0, 0], f_rsem.at[0, 0], peer(zh, right, core)))
-    own_l[1].wait_recv()
+    came(own_l, 1)
     src = kv_ref.at[zh * 4 + right, other]
     far_l = go(remote(src, src, f_ssem.at[0, 1], f_rsem.at[0, 1], peer(zh, left, core)))
-    for copy in q_copies[3:]:
-        copy.start()
-    own_r[1].wait_recv()
-    own_l[0].wait_recv()
+    came(own_r, 1)
+    came(own_l, 0)
     z_r[0].wait_recv()
     src = kv_ref.at[(1 - zh) * 4 + left, core]
     zfar_r = go(remote(src, src, f_ssem.at[1, 0], f_rsem.at[1, 0], peer(zh, right, core)))
@@ -222,25 +248,14 @@
     src = kv_ref.at[(1 - zh) * 4 + right, other]
     zfar_l = go(remote(src, src, f_ssem.at[1, 1], f_rsem.at[1, 1], peer(zh, left, core)))
 
-    def half_cols(ref, side):
-        return ref.at[:, :, pl.ds(pl.multiple_of(side * HALF, HALF), HALF)]
-
-    send_self = pltpu.make_async_copy(send_q.at[0], q_land.at[0], local_sem.at[3])
-    send_self.start()
-    send_self.wait()
-    for copy in q_copies:
-        copy.wait_recv()
-        sends.append(copy)
-    q_swap = go(remote(half_cols(q_land, other), rq_ref.at[core], q_ssem.at[0], q_rsem.at[0], peer(zh, x, other)))
-    q_here = pltpu.make_async_copy(half_cols(q_land, core), rq_ref.at[core], local_sem.at[4])
-    q_here.start()
     z_r[1].wait_recv()
     z_l[0].wait_recv()
     own_c.wait_recv()
     do_copy.wait_recv()
     for copy in (far_r, far_l, zfar_r, zfar_l):
         copy.wait_recv()
-    q_swap.wait_recv()
+    for copy in q_copies:
+        copy.wait_recv()
     q_here.wait()
     own_do.wait()
     own_here.wait()
@@ -534,12 +549,11 @@
             pltpu.VMEM((GROUPS, BLOCK, 2 * HALF), low),
             pltpu.VMEM((2, GROUPS, BLOCK, 2 * KEYS_HALF), low),
             pltpu.VMEM((2, GROUPS, BLOCK, 2 * KEYS_HALF), low),
-            pltpu.VMEM((GROUPS, BLOCK, 2 * HALF), low),
             dma((6,)),
             dma((GROUPS,)), dma((GROUPS,)),
-            dma((GROUPS,)), dma((GROUPS,)),
+            dma((GROUPS, 2)), dma((GROUPS, 2)),
             dma, dma,
-            dma((4, 2)), dma((4, 2)),
+            dma((3, 2, 2)), dma((3, 2, 2)), dma((2,)),
             dma((2, 2)), dma((2, 2)),
             dma((2, 2)), dma((2, 2)),
             dma((5,)),

time: 81.9 us -> 79.1 us (0.966)
  Pallas kernels: 80.8 us -> 78.2 us
    pallas_call x1, Pallas kernels: 39.2 us -> 34.6 us  [on_device(): pl.pallas_call(gather_kernel, out_shape=(jax.ShapeDtypeStruct((2, GROUPS,...]
    pallas_call x1, Pallas kernels: 16.6 us -> 17.9 us  [on_device(): pl.pallas_call(attend_kernel, out_shape=(jax.ShapeDtypeStruct((2 * ROWS,...]
where the time goes in v3:
time: 79.1 us; the launch traced here: 78.9 us
  Pallas kernels  78.2 us (99%)
    pallas_call x1, Pallas kernels, on_device(): pl.pallas_call(gather_kernel, out_shape=(jax.ShapeDtypeStruct((2, GROUPS,...  34.6 us
    pallas_call x1, Pallas kernels, on_device(): pl.pallas_call(scatter_kernel, out_shape=(jax.ShapeDtypeStruct((ROWS, HAL...  23.2 us
    pallas_call x1, Pallas kernels, on_device(): pl.pallas_call(attend_kernel, out_shape=(jax.ShapeDtypeStruct((2 * ROWS,...  17.9 us
    pallas_call x1, Pallas kernels, on_device(): pl.pallas_call(finish_kernel, out_shape=(jax.ShapeDtypeStruct((ROWS, 2 *...  2.55 us

profile of v3, /device:TPU:1, one launch (start us, length us, event | category | flops | bytes accessed | tf_op | source)
XLA Modules:
  0.0 78.9 jit_solution(387670024467237326)
XLA Ops:
  0.6 34.6 %move_and_gather.1 = (bf16[2,8,16,2048]{3,2,1,0:T(8,128)(2,1)}, bf16[2,128,2048]{2,1,0:T(8,128)(2,1)}, bf16[8,2,8,16,512]{4,3,2,1,0:T(8,128)(2,1)}, s32[256]{0:T(256)}) custom-call(bf16[8,16,4096]{2,1,0:T(8,128)(2,1)} %bitcast.18, bf16[8,16,512]{2,1,0:T(8,128)(2,1)} %bitcast.19, bf16[8,16,512]{2,1,0:T(8,128)(2,1)} %bitcast.20, bf16[128,4096]{1,0:T(8,128)(2,1)} %do_ref.1, ...), custom_call_target="tpu_custom_call" | custom-call | tf_op jit(solution)/shard_map/move_and_gather/pallas_call | solution.py:531
  35.2 17.9 %attend.1 = (bf16[256,2048]{1,0:T(8,128)(2,1)}, bf16[256,2048]{1,0:T(8,128)(2,1)}, bf16[128,16,512]{2,1,0:T(8,128)(2,1)}) custom-call(s32[256]{0:T(256)} %get-tuple-element.14.table_ref, s32[8,8]{1,0:T(8,128)} %lengths_ref.1, s32[8,128]{1,0:T(8,128)} %order_ref.1, bf16[256,2048]{1,0:T(8,128)(2,1)} %bitcast.16, bf16[256,2048]{1,0:T(8,128)(2,1)} %bitcast.17, ...), custom_call_target="tpu_custom_call" | custom-call | tf_op jit(solution)/shard_map/attend/pallas_call | solution.py:568
  53.2 23.2 %reduce_and_share.1 = (bf16[128,2048]{1,0:T(8,128)(2,1)}, bf16[128,2048]{1,0:T(8,128)(2,1)}, bf16[2,128,512]{2,1,0:T(8,128)(2,1)}) custom-call(bf16[2,128,2048]{2,1,0:T(8,128)(2,1)} %bitcast.10, bf16[2,128,2048]{2,1,0:T(8,128)(2,1)} %bitcast.12, bf16[8,2,128,512]{3,2,1,0:T(8,128)(2,1)} %bitcast.15), custom_call_target="tpu_custom_call" | custom-call | tf_op jit(solution)/shard_map/reduce_and_share/pallas_call | solution.py:598
  76.4 2.6 %finish.1 = (bf16[128,4096]{1,0:T(8,128)(2,1)}, bf16[128,4096]{1,0:T(8,128)(2,1)}, bf16[128,512]{1,0:T(8,128)(2,1)}, bf16[128,512]{1,0:T(8,128)(2,1)}) custom-call(bf16[2,128,2048]{2,1,0:T(8,128)(2,1)} %bitcast.11, bf16[2,128,2048]{2,1,0:T(8,128)(2,1)} %bitcast.13, bf16[128,2048]{1,0:T(8,128)(2,1)} %get-tuple-element.21.attn_in, ...), custom_call_target="tpu_custom_call" | custom-call | tf_op jit(solution)/shard_map/finish/pallas_call | solution.py:626

commit v4 on v3

--- a/solution.py
+++ b/solution.py
@@ -265,7 +265,7 @@
 
 def attend_kernel(
     table_ref, lengths_ref, order_ref, rq_hbm, do_hbm, kv_hbm,
-    attn_hbm, dq_hbm, dkv_hbm,
+    attn_full, dq_full, attn_send, dq_send, dkv_hbm,
     rq_ref, do_ref, kv_ref, attn_ref, dq_ref, dkv_ref, ks, acc, turned, in_sem, out_sem,
 ):
     group = lax.axis_index("dp")
@@ -384,8 +384,15 @@
         return carry
 
     lax.fori_loop(0, 2 * GROUPS // TOGETHER, item, 0)
+    core = lax.axis_index("fsdp") % 2
+    cols = pl.ds(pl.multiple_of(core * HALF, HALF), HALF)
+    kept = pl.ds(pl.multiple_of(core * ROWS, ROWS), ROWS)
+    sent = pl.ds(pl.multiple_of((1 - core) * ROWS, ROWS), ROWS)
     stores = [
-        pltpu.make_async_copy(attn_ref, attn_hbm, out_sem.at[0]), pltpu.make_async_copy(dq_ref, dq_hbm, out_sem.at[1])
+        pltpu.make_async_copy(attn_ref.at[sent], attn_send, out_sem.at[0]),
+        pltpu.make_async_copy(dq_ref.at[sent], dq_send, out_sem.at[1]),
+        pltpu.make_async_copy(attn_ref.at[kept], attn_full.at[:, cols], out_sem.at[2]),
+        pltpu.make_async_copy(dq_ref.at[kept], dq_full.at[:, cols], out_sem.at[3]),
     ]
     for copy in stores:
         copy.start()
@@ -406,7 +413,7 @@
 
     for i, piece in enumerate(pieces):
         lax.fori_loop(i * SLOTS // PIECES, (i + 1) * SLOTS // PIECES, restore, 0, unroll=8)
-        copy = pltpu.make_async_copy(dkv_ref.at[piece], dkv_hbm.at[piece], out_sem.at[2 + i])
+        copy = pltpu.make_async_copy(dkv_ref.at[piece], dkv_hbm.at[piece], out_sem.at[4 + i])
         copy.start()
         stores.append(copy)
     for copy in stores:
@@ -414,7 +421,7 @@
 
 
 def scatter_kernel(
-    attn2_ref, dq2_ref, u_hbm,
+    attn_send, dq_send, u_hbm,
     attn_ref, dq_ref, grads_ref,
     u_ref, z0_in, far_out, far_in, cross_in, near_out, near_in, z1_out, z1_in, total,
     o_ssem, o_rsem, z_ssem, z_rsem, f_ssem, f_rsem, c_ssem, c_rsem, n_ssem, n_rsem, local_sem, u_sem,
@@ -447,29 +454,42 @@
 
     here, there = zh * 4, (1 - zh) * 4
     sides = ((0, r_peer, right), (1, l_peer, left))
-    z0 = go(u_hbm.at[there + across], z0_in, z_ssem.at[0], z_rsem.at[0], z_peer)
+    parts = [pl.ds(i * ROWS // 2, ROWS // 2) for i in range(2)]
+    z0 = {
+        (q, d): go(
+            u_hbm.at[there + across, d, parts[q]], z0_in.at[d, parts[q]], z_ssem.at[2 * q + d], z_rsem.at[2 * q + d], z_peer
+        )
+        for q in range(2) for d in range(2)
+    }
     cross = [go(u_hbm.at[there + to], cross_in.at[d], c_ssem.at[d], c_rsem.at[d], dev) for d, dev, to in sides]
     outs = [
-        go(src.at[other], dst, o_ssem.at[i], o_rsem.at[i], core_peer)
-        for i, (src, dst) in enumerate(((attn2_ref, attn_ref), (dq2_ref, dq_ref)))
+        go(src, dst, o_ssem.at[i], o_rsem.at[i], core_peer)
+        for i, (src, dst) in enumerate(((attn_send, attn_ref), (dq_send, dq_ref)))
     ]
     u_load.wait()
-    z0.wait_recv()
-    far = []
-    for d, dev, to in sides:
-        far_out[d] = (wide(u_ref[here + across, d]) + wide(z0_in[d])).astype(jnp.bfloat16)
-        far.append(go(far_out.at[d], far_in.at[d], f_ssem.at[d], f_rsem.at[d], dev))
-    near = []
+    far, near = {}, []
+
+    def send_far(q):
+        for d, dev, to in sides:
+            z0[q, d].wait_recv()
+            far_out[d, parts[q]] = (wide(u_ref[here + across, d, parts[q]]) + wide(z0_in[d, parts[q]])).astype(jnp.bfloat16)
+            far[q, d] = go(far_out.at[d, parts[q]], far_in.at[d, parts[q]], f_ssem.at[d, q], f_rsem.at[d, q], dev)
+
+    send_far(0)
     for d, dev, to in sides:
         near.append(go(u_ref.at[here + to, 1 - d], near_in.at[d, 1 - d], n_ssem.at[d, 0], n_rsem.at[d, 0], dev))
     for copy in cross:
         copy.wait_recv()
     z1_out[...] = (wide(u_ref[there + x]) + wide(cross_in[0]) + wide(cross_in[1])).astype(jnp.bfloat16)
-    z1 = go(z1_out, z1_in, z_ssem.at[1], z_rsem.at[1], z_peer)
-    for d, dev, to in sides:
-        far[d].wait_recv()
-        near_out[d] = (wide(u_ref[here + to, d]) + wide(far_in[d])).astype(jnp.bfloat16)
-        near.append(go(near_out.at[d], near_in.at[d, d], n_ssem.at[d, 1], n_rsem.at[d, 1], dev))
+    z1 = go(z1_out, z1_in, z_ssem.at[4], z_rsem.at[4], z_peer)
+    send_far(1)
+    for q in range(2):
+        for d, dev, to in sides:
+            far[q, d].wait_recv()
+            near_out[d, parts[q]] = (wide(u_ref[here + to, d, parts[q]]) + wide(far_in[d, parts[q]])).astype(jnp.bfloat16)
+            near.append(go(
+                near_out.at[d, parts[q]], near_in.at[d, d, parts[q]], n_ssem.at[d, 1 + q], n_rsem.at[d, 1 + q], dev
+            ))
     z1.wait_recv()
     for copy in near:
         copy.wait_recv()
@@ -488,7 +508,7 @@
 
 
 def finish_kernel(
-    attn2_ref, dq2_ref, attn_in, dq_in, grads_in, attn_ref, dq_ref, gk_ref, gv_ref, wide, narrow, in_sem, out_sem,
+    attn_full, dq_full, attn_in, dq_in, grads_in, attn_ref, dq_ref, gk_ref, gv_ref, wide, narrow, in_sem, out_sem,
 ):
     core = lax.axis_index("fsdp") % 2
 
@@ -500,10 +520,8 @@
             (narrow.at[side, :, pl.ds(which * KEYS_HALF, KEYS_HALF)], cols(dst, side, KEYS_HALF))
             for side in range(2) for which, dst in enumerate((gk_ref, gv_ref))
         ]),
-        (attn2_ref.at[core], wide.at[0], [(wide.at[0], cols(attn_ref, core, HALF))]),
-        (dq2_ref.at[core], wide.at[1], [(wide.at[1], cols(dq_ref, core, HALF))]),
-        (attn_in, wide.at[2], [(wide.at[2], cols(attn_ref, 1 - core, HALF))]),
-        (dq_in, wide.at[3], [(wide.at[3], cols(dq_ref, 1 - core, HALF))]),
+        (attn_in, wide.at[0], [(wide.at[0], cols(attn_ref, 1 - core, HALF))]),
+        (dq_in, wide.at[1], [(wide.at[1], cols(dq_ref, 1 - core, HALF))]),
     ]
     loads = [pltpu.make_async_copy(src, here, in_sem.at[i]) for i, (src, here, _) in enumerate(groups)]
     for copy in loads:
@@ -565,15 +583,17 @@
         values.reshape(GROUPS, BLOCK, 2 * KEYS_HALF), output_gradient, group_shift.T, block_order, doc_lengths,
     )
 
-    attn2, dq2, dkv = pl.pallas_call(
+    attn_full, dq_full, attn_send, dq_send, dkv = pl.pallas_call(
         attend_kernel,
         out_shape=(
-            jax.ShapeDtypeStruct((2 * ROWS, HALF), low),
-            jax.ShapeDtypeStruct((2 * ROWS, HALF), low),
+            jax.ShapeDtypeStruct((ROWS, 2 * HALF), low),
+            jax.ShapeDtypeStruct((ROWS, 2 * HALF), low),
+            jax.ShapeDtypeStruct((ROWS, HALF), low),
+            jax.ShapeDtypeStruct((ROWS, HALF), low),
             jax.ShapeDtypeStruct((SLOTS, BLOCK, 2 * KEYS_HALF), low),
         ),
         in_specs=[SMEM, SMEM, SMEM, ANY, ANY, ANY],
-        out_specs=(ANY, ANY, ANY),
+        out_specs=(ANY,) * 5,
         scratch_shapes=[
             pltpu.VMEM((2 * ROWS, HALF), low), pltpu.VMEM((2 * ROWS, HALF), low),
             pltpu.VMEM((SLOTS, BLOCK, 2 * KEYS_HALF), low),
@@ -582,7 +602,7 @@
             pltpu.VMEM((GROUP_ROWS, 2 * KEYS_HALF), low),
             pltpu.VMEM((2, 2, HEAD, GROUP_ROWS), jnp.float32),
             pltpu.VMEM((GROUP_ROWS, 2 * KEYS_HALF), low),
-            dma((2 + PIECES,)), dma((2 + PIECES,)),
+            dma((2 + PIECES,)), dma((4 + PIECES,)),
         ],
         compiler_params=pltpu.CompilerParams(vmem_limit_bytes=WHOLE),
         name="attend",
@@ -591,8 +611,6 @@
         rq.reshape(2 * ROWS, HALF), do2.reshape(2 * ROWS, HALF),
         kv.reshape(SLOTS, BLOCK, 2 * KEYS_HALF),
     )
-    attn2 = attn2.reshape(2, ROWS, HALF)
-    dq2 = dq2.reshape(2, ROWS, HALF)
 
     region = (2, ROWS, 2 * KEYS_HALF)
     attn_in, dq_in, grads = pl.pallas_call(
@@ -613,15 +631,15 @@
             pltpu.VMEM(region, low), pltpu.VMEM(region, low),
             pltpu.VMEM(region, low),
             dma((3,)), dma((3,)),
+            dma((5,)), dma((5,)),
+            dma((2, 2)), dma((2, 2)),
             dma((2,)), dma((2,)),
-            dma((2,)), dma((2,)),
-            dma((2,)), dma((2,)),
-            dma((2, 2)), dma((2, 2)),
+            dma((2, 3)), dma((2, 3)),
             dma, dma,
         ],
         compiler_params=pltpu.CompilerParams(collective_id=2, has_side_effects=True, vmem_limit_bytes=WHOLE),
         name="reduce_and_share",
-    )(attn2, dq2, dkv.reshape((CHIPS,) + region))
+    )(attn_send, dq_send, dkv.reshape((CHIPS,) + region))
 
     return pl.pallas_call(
         finish_kernel,
@@ -633,10 +651,11 @@
         ),
         in_specs=[ANY] * 5,
         out_specs=(ANY,) * 4,
-        scratch_shapes=[pltpu.VMEM((4, ROWS, HALF), low), pltpu.VMEM(region, low), dma((5,)), dma((8,))],
+        scratch_shapes=[pltpu.VMEM((2, ROWS, HALF), low), pltpu.VMEM(region, low), dma((3,)), dma((6,))],
+        input_output_aliases={0: 0, 1: 1},
         compiler_params=pltpu.CompilerParams(vmem_limit_bytes=WHOLE),
         name="finish",
-    )(attn2, dq2, attn_in, dq_in, grads)
+    )(attn_full, dq_full, attn_in, dq_in, grads)
 
 
 def solution(mesh):

time: 79.1 us -> 78 us (0.986)
  Pallas kernels: 78.2 us -> 77.1 us
    pallas_call x1, Pallas kernels: 23.2 us -> 22.2 us  [on_device(): pl.pallas_call(scatter_kernel, out_shape=(jax.ShapeDtypeStruct((ROWS, HAL...]
where the time goes in v4:
time: 78 us; the launch traced here: 77.8 us
  Pallas kernels  77.1 us (99%)
    pallas_call x1, Pallas kernels, on_device(): pl.pallas_call(gather_kernel, out_shape=(jax.ShapeDtypeStruct((2, GROUPS,...  34.6 us
    pallas_call x1, Pallas kernels, on_device(): pl.pallas_call(scatter_kernel, out_shape=(jax.ShapeDtypeStruct((ROWS, HAL...  22.2 us
    pallas_call x1, Pallas kernels, on_device(): pl.pallas_call(attend_kernel, out_shape=(jax.ShapeDtypeStruct((ROWS, 2 *...  18.1 us
    pallas_call x1, Pallas kernels, on_device(): pl.pallas_call(finish_kernel, out_shape=(jax.ShapeDtypeStruct((ROWS, 2 *...  2.17 us

profile of v4, /device:TPU:1, one launch (start us, length us, event | category | flops | bytes accessed | tf_op | source)
XLA Modules:
  0.0 77.8 jit_solution(14248044393228280242)
XLA Ops:
  0.6 34.6 %move_and_gather.1 = (bf16[2,8,16,2048]{3,2,1,0:T(8,128)(2,1)}, bf16[2,128,2048]{2,1,0:T(8,128)(2,1)}, bf16[8,2,8,16,512]{4,3,2,1,0:T(8,128)(2,1)}, s32[256]{0:T(256)}) custom-call(bf16[8,16,4096]{2,1,0:T(8,128)(2,1)} %bitcast.12, bf16[8,16,512]{2,1,0:T(8,128)(2,1)} %bitcast.13, bf16[8,16,512]{2,1,0:T(8,128)(2,1)} %bitcast.14, bf16[128,4096]{1,0:T(8,128)(2,1)} %do_ref.1, ...), custom_call_target="tpu_custom_call" | custom-call | tf_op jit(solution)/shard_map/move_and_gather/pallas_call | solution.py:549
  35.2 18.1 %attend.1 = (bf16[128,4096]{1,0:T(8,128)(2,1)}, bf16[128,4096]{1,0:T(8,128)(2,1)}, bf16[128,2048]{1,0:T(8,128)(2,1)}, bf16[128,2048]{1,0:T(8,128)(2,1)}, bf16[128,16,512]{2,1,0:T(8,128)(2,1)}) custom-call(s32[256]{0:T(256)} %get-tuple-element.16.table_ref, s32[8,8]{1,0:T(8,128)} %lengths_ref.1, s32[8,128]{1,0:T(8,128)} %order_ref.1, ...), custom_call_target="tpu_custom_call" | custom-call | tf_op jit(solution)/shard_map/attend/pallas_call | solution.py:586
  53.3 22.2 %reduce_and_share.1 = (bf16[128,2048]{1,0:T(8,128)(2,1)}, bf16[128,2048]{1,0:T(8,128)(2,1)}, bf16[2,128,512]{2,1,0:T(8,128)(2,1)}) custom-call(bf16[128,2048]{1,0:T(8,128)(2,1)} %get-tuple-element.22.attn_send, bf16[128,2048]{1,0:T(8,128)(2,1)} %get-tuple-element.23.dq_send, bf16[8,2,128,512]{3,2,1,0:T(8,128)(2,1)} %bitcast.9), custom_call_target="tpu_custom_call" | custom-call | tf_op jit(solution)/shard_map/reduce_and_share/pallas_call | solution.py:616
  75.6 2.2 %finish.1 = (bf16[128,4096]{1,0:T(8,128)(2,1)}, bf16[128,4096]{1,0:T(8,128)(2,1)}, bf16[128,512]{1,0:T(8,128)(2,1)}, bf16[128,512]{1,0:T(8,128)(2,1)}) custom-call(bf16[128,4096]{1,0:T(8,128)(2,1)} %get-tuple-element.20.attn_full, bf16[128,4096]{1,0:T(8,128)(2,1)} %get-tuple-element.21.dq_full, ...), custom_call_target="tpu_custom_call", output_to_operand_aliasing={{0}: (0, {}), {1}: (1, {})} | custom-call | tf_op jit(solution)/shard_map/finish/pallas_call | solution.py:644

commit v5 on v4

--- a/solution.py
+++ b/solution.py
@@ -404,7 +404,7 @@
                 turned[keys, pl.ds(which * KEYS_HALF + h * HEAD, HEAD)] = acc[h, which, :, keys].T.astype(jnp.bfloat16)
         return carry
 
-    lax.fori_loop(0, GROUP_ROWS // CHUNK, turn, 0)
+    lax.fori_loop(0, GROUP_ROWS // CHUNK, turn, 0, unroll=4)
 
     def restore(slot, carry):
         src = pl.multiple_of(order_ref[group, slot] * BLOCK, BLOCK)
@@ -493,10 +493,15 @@
     z1.wait_recv()
     for copy in near:
         copy.wait_recv()
-    total[...] = (
-        wide(u_ref[here + x]) + wide(z1_in[...]) + wide(near_in[0]) + wide(near_in[1])
-    ).astype(jnp.bfloat16)
+
+    def add_up(side):
+        total[side] = (
+            wide(u_ref[here + x, side]) + wide(z1_in[side]) + wide(near_in[0, side]) + wide(near_in[1, side])
+        ).astype(jnp.bfloat16)
+
+    add_up(other)
     last = go(total.at[other], grads_ref.at[core], o_ssem.at[2], o_rsem.at[2], core_peer)
+    add_up(core)
     kept = pltpu.make_async_copy(total.at[core], grads_ref.at[core], local_sem)
     kept.start()
     for copy in outs:

time: 78 us -> 76.7 us (0.983); the launches traced: 77.8 us -> 75.6 us
  Pallas kernels: 77.1 us -> 74.9 us
    pallas_call x1, Pallas kernels: 18.1 us -> 17 us  [on_device(): pl.pallas_call(attend_kernel, out_shape=(jax.ShapeDtypeStruct((ROWS, 2 *...]
    pallas_call x1, Pallas kernels: 22.2 us -> 21.2 us  [on_device(): pl.pallas_call(scatter_kernel, out_shape=(jax.ShapeDtypeStruct((ROWS, HAL...]
where the time goes in v5:
time: 76.7 us; the launch traced here: 75.6 us
  Pallas kernels  74.9 us (98%)
    pallas_call x1, Pallas kernels, on_device(): pl.pallas_call(gather_kernel, out_shape=(jax.ShapeDtypeStruct((2, GROUPS,...  34.6 us
    pallas_call x1, Pallas kernels, on_device(): pl.pallas_call(scatter_kernel, out_shape=(jax.ShapeDtypeStruct((ROWS, HAL...  21.2 us
    pallas_call x1, Pallas kernels, on_device(): pl.pallas_call(attend_kernel, out_shape=(jax.ShapeDtypeStruct((ROWS, 2 *...  17 us
    pallas_call x1, Pallas kernels, on_device(): pl.pallas_call(finish_kernel, out_shape=(jax.ShapeDtypeStruct((ROWS, 2 *...  2.17 us

profile of v5, /device:TPU:1, one launch (start us, length us, event | category | flops | bytes accessed | tf_op | source)
XLA Modules:
  0.0 75.6 jit_solution(3525596867110265080)
XLA Ops:
  0.6 34.6 %move_and_gather.1 = (bf16[2,8,16,2048]{3,2,1,0:T(8,128)(2,1)}, bf16[2,128,2048]{2,1,0:T(8,128)(2,1)}, bf16[8,2,8,16,512]{4,3,2,1,0:T(8,128)(2,1)}, s32[256]{0:T(256)}) custom-call(bf16[8,16,4096]{2,1,0:T(8,128)(2,1)} %bitcast.12, bf16[8,16,512]{2,1,0:T(8,128)(2,1)} %bitcast.13, bf16[8,16,512]{2,1,0:T(8,128)(2,1)} %bitcast.14, bf16[128,4096]{1,0:T(8,128)(2,1)} %do_ref.1, ...), custom_call_target="tpu_custom_call" | custom-call | tf_op jit(solution)/shard_map/move_and_gather/pallas_call | solution.py:554
  35.2 17.0 %attend.1 = (bf16[128,4096]{1,0:T(8,128)(2,1)}, bf16[128,4096]{1,0:T(8,128)(2,1)}, bf16[128,2048]{1,0:T(8,128)(2,1)}, bf16[128,2048]{1,0:T(8,128)(2,1)}, bf16[128,16,512]{2,1,0:T(8,128)(2,1)}) custom-call(s32[256]{0:T(256)} %get-tuple-element.16.table_ref, s32[8,8]{1,0:T(8,128)} %lengths_ref.1, s32[8,128]{1,0:T(8,128)} %order_ref.1, ...), custom_call_target="tpu_custom_call" | custom-call | tf_op jit(solution)/shard_map/attend/pallas_call | solution.py:591
  52.2 21.2 %reduce_and_share.1 = (bf16[128,2048]{1,0:T(8,128)(2,1)}, bf16[128,2048]{1,0:T(8,128)(2,1)}, bf16[2,128,512]{2,1,0:T(8,128)(2,1)}) custom-call(bf16[128,2048]{1,0:T(8,128)(2,1)} %get-tuple-element.22.attn_send, bf16[128,2048]{1,0:T(8,128)(2,1)} %get-tuple-element.23.dq_send, bf16[8,2,128,512]{3,2,1,0:T(8,128)(2,1)} %bitcast.9), custom_call_target="tpu_custom_call" | custom-call | tf_op jit(solution)/shard_map/reduce_and_share/pallas_call | solution.py:621
  73.4 2.2 %finish.1 = (bf16[128,4096]{1,0:T(8,128)(2,1)}, bf16[128,4096]{1,0:T(8,128)(2,1)}, bf16[128,512]{1,0:T(8,128)(2,1)}, bf16[128,512]{1,0:T(8,128)(2,1)}) custom-call(bf16[128,4096]{1,0:T(8,128)(2,1)} %get-tuple-element.20.attn_full, bf16[128,4096]{1,0:T(8,128)(2,1)} %get-tuple-element.21.dq_full, ...), custom_call_target="tpu_custom_call", output_to_operand_aliasing={{0}: (0, {}), {1}: (1, {})} | custom-call | tf_op jit(solution)/shard_map/finish/pallas_call | solution.py:649

commit v6 on v5

--- a/solution.py
+++ b/solution.py
@@ -159,9 +159,9 @@
             kv_copies[arrived].wait_recv()
             arrived += 1
         for f in range(2):
-            own_z[f, part] = own_send(0, f, part, (1 - zh, x))
             own_r[f, part] = own_send(1, f, part, (zh, right))
             own_l[f, part] = own_send(2, f, part, (zh, left))
+            own_z[f, part] = own_send(0, f, part, (1 - zh, x))
     q_copies = [q_send(slot, flip) for slot in range(1, 4) for flip in range(2)]
     own_c = go(remote(own.at[other], kv_ref.at[chip, core], c_sem.at[0], c_sem.at[1], peer(zh, x, other)))
     own_here = pltpu.make_async_copy(own.at[core], kv_ref.at[chip, core], local_sem.at[1])
@@ -360,7 +360,7 @@
                 d['dos'], d['wl'], (((0,), (0,)), ((), ())), preferred_element_type=jnp.float32
             )
         for d in chains:
-            d['ds'] = (d['w'] * (d['dp'] - d['delta'])).astype(jnp.bfloat16)
+            d['ds'] = d['wl'] * (d['dp'] - d['delta']).astype(jnp.bfloat16)
         for d in chains:
             gq = lax.dot_general(d['ds'], d['k'](), (((1,), (0,)), ((), ())), preferred_element_type=jnp.float32)
             d['gq'] = (gq * (d['inv'] * SCALE)).astype(jnp.bfloat16)

time: 76.7 us -> 76.9 us (level); the launches traced: 75.6 us -> 77.1 us
  Pallas kernels: 74.9 us -> 76.4 us
    pallas_call x1, Pallas kernels: 21.2 us -> 22.5 us  [on_device(): pl.pallas_call(scatter_kernel, out_shape=(jax.ShapeDtypeStruct((ROWS, HAL...]
where the time goes in v6:
time: 76.9 us; the launch traced here: 77.1 us
  Pallas kernels  76.4 us (99%)
    pallas_call x1, Pallas kernels, on_device(): pl.pallas_call(gather_kernel, out_shape=(jax.ShapeDtypeStruct((2, GROUPS,...  34.6 us
    pallas_call x1, Pallas kernels, on_device(): pl.pallas_call(scatter_kernel, out_shape=(jax.ShapeDtypeStruct((ROWS, HAL...  22.5 us
    pallas_call x1, Pallas kernels, on_device(): pl.pallas_call(attend_kernel, out_shape=(jax.ShapeDtypeStruct((ROWS, 2 *...  17.2 us
    pallas_call x1, Pallas kernels, on_device(): pl.pallas_call(finish_kernel, out_shape=(jax.ShapeDtypeStruct((ROWS, 2 *...  2.17 us

profile of v6, /device:TPU:1, one launch (start us, length us, event | category | flops | bytes accessed | tf_op | source)
XLA Modules:
  0.0 77.1 jit_solution(8633302131314325523)
XLA Ops:
  0.6 34.6 %move_and_gather.1 = (bf16[2,8,16,2048]{3,2,1,0:T(8,128)(2,1)}, bf16[2,128,2048]{2,1,0:T(8,128)(2,1)}, bf16[8,2,8,16,512]{4,3,2,1,0:T(8,128)(2,1)}, s32[256]{0:T(256)}) custom-call(bf16[8,16,4096]{2,1,0:T(8,128)(2,1)} %bitcast.12, bf16[8,16,512]{2,1,0:T(8,128)(2,1)} %bitcast.13, bf16[8,16,512]{2,1,0:T(8,128)(2,1)} %bitcast.14, bf16[128,4096]{1,0:T(8,128)(2,1)} %do_ref.1, ...), custom_call_target="tpu_custom_call" | custom-call | tf_op jit(solution)/shard_map/move_and_gather/pallas_call | solution.py:554
  35.2 17.2 %attend.1 = (bf16[128,4096]{1,0:T(8,128)(2,1)}, bf16[128,4096]{1,0:T(8,128)(2,1)}, bf16[128,2048]{1,0:T(8,128)(2,1)}, bf16[128,2048]{1,0:T(8,128)(2,1)}, bf16[128,16,512]{2,1,0:T(8,128)(2,1)}) custom-call(s32[256]{0:T(256)} %get-tuple-element.16.table_ref, s32[8,8]{1,0:T(8,128)} %lengths_ref.1, s32[8,128]{1,0:T(8,128)} %order_ref.1, ...), custom_call_target="tpu_custom_call" | custom-call | tf_op jit(solution)/shard_map/attend/pallas_call | solution.py:591
  52.5 22.5 %reduce_and_share.1 = (bf16[128,2048]{1,0:T(8,128)(2,1)}, bf16[128,2048]{1,0:T(8,128)(2,1)}, bf16[2,128,512]{2,1,0:T(8,128)(2,1)}) custom-call(bf16[128,2048]{1,0:T(8,128)(2,1)} %get-tuple-element.22.attn_send, bf16[128,2048]{1,0:T(8,128)(2,1)} %get-tuple-element.23.dq_send, bf16[8,2,128,512]{3,2,1,0:T(8,128)(2,1)} %bitcast.9), custom_call_target="tpu_custom_call" | custom-call | tf_op jit(solution)/shard_map/reduce_and_share/pallas_call | solution.py:621
  74.9 2.2 %finish.1 = (bf16[128,4096]{1,0:T(8,128)(2,1)}, bf16[128,4096]{1,0:T(8,128)(2,1)}, bf16[128,512]{1,0:T(8,128)(2,1)}, bf16[128,512]{1,0:T(8,128)(2,1)}) custom-call(bf16[128,4096]{1,0:T(8,128)(2,1)} %get-tuple-element.20.attn_full, bf16[128,4096]{1,0:T(8,128)(2,1)} %get-tuple-element.21.dq_full, ...), custom_call_target="tpu_custom_call", output_to_operand_aliasing={{0}: (0, {}), {1}: (1, {})} | custom-call | tf_op jit(solution)/shard_map/finish/pallas_call | solution.py:649
